TPU v7x, 128 devices: a whole 4x4x4 slice. The times are simulated.
128 devices in a mesh: rows: 2 (over y_hi), vocab: 64 (over x, z, y_lo, core).
Axes of the slice: x: 4, y: 4 (y_hi: 2, y_lo: 2; y = y_hi * 2 + y_lo), z: 4, core: 2. Of those that a mesh axis runs over, the one named last changes fastest.
Arguments:
- teacher_hidden: bfloat16 [1536, 4096], P('rows'), may hold values from -240 to 240
- teacher_head: bfloat16 [4096, 81920], P(None, 'vocab'), may hold values from -0.25 to 0.25
- student_hidden: bfloat16 [1536, 3584], P('rows', 'vocab'), may hold values from -240 to 240
- student_head: bfloat16 [3584, 81920], P(None, 'vocab'), may hold values from -0.3125 to 0.3125
- token_ids: int32 [1536], P('rows'), may hold values from 0 to 81919
- response_mask: int32 [1536], P('rows'), may hold values from 0 to 1, as said below
Outputs:
- kl_loss: float32 [], replicated
- hidden_grad: bfloat16 [1536, 3584], P('rows', 'vocab')
Inputs may be any that keep to these rules, and one draw needn't show every extreme that they name: `response_mask`: the last row of each aligned block of 8 rows is a response row.
All inputs are finite; a program needn't handle non-finite values.
Results may differ from a plain program's by a relative error of at most 0.0046.
Values may be sent and summed in bfloat16 or wider, within the bound.
A program may use at most 128 MiB of HBM per device.

v0:
```python
import jax
import jax.numpy as jnp
from jax import lax
from jax.sharding import PartitionSpec as P

CE_WEIGHT = 0.5


def local(teacher_hidden, teacher_head, student_hidden, student_head, token_ids, response_mask):
    shard_cols = teacher_head.shape[1]
    row_count = teacher_hidden.shape[0]
    weights = response_mask.astype(jnp.float32)
    masked = lax.psum(jnp.sum(weights), "rows")
    teacher_logits = jnp.dot(teacher_hidden, teacher_head, preferred_element_type=jnp.float32)
    whole_hidden = lax.all_gather(student_hidden, "vocab", axis=1, tiled=True)
    student_logits = jnp.dot(whole_hidden, student_head, preferred_element_type=jnp.float32)
    first_col = lax.axis_index("vocab") * shard_cols
    columns = first_col + lax.broadcasted_iota(jnp.int32, (row_count, shard_cols), 1)
    chosen = columns == token_ids[:, None]
    target_local = jnp.sum(jnp.where(chosen, student_logits, 0.0), axis=1)
    difference = teacher_logits - student_logits
    t_max, s_max = lax.pmax(
        (jnp.max(teacher_logits, axis=1), jnp.max(student_logits, axis=1)), "vocab"
    )
    t_exp = jnp.exp(teacher_logits - t_max[:, None])
    s_exp = jnp.exp(student_logits - s_max[:, None])
    t_sum, cross_sum, s_sum, target = lax.psum(
        (
            jnp.sum(t_exp, axis=1),
            jnp.sum(t_exp * difference, axis=1),
            jnp.sum(s_exp, axis=1),
            target_local,
        ),
        "vocab",
    )
    teacher_lse = t_max + jnp.log(t_sum)
    student_lse = s_max + jnp.log(s_sum)
    row_kl = cross_sum / t_sum - teacher_lse + student_lse
    row_nll = student_lse - target
    loss_local = jnp.sum(weights * (row_kl + CE_WEIGHT * row_nll))
    kl_loss = lax.psum(loss_local, "rows") / masked
    teacher_prob = jnp.exp(teacher_logits - teacher_lse[:, None])
    student_prob = jnp.exp(student_logits - student_lse[:, None])
    row_scale = weights / masked
    logit_grad = (
        row_scale[:, None]
        * ((1.0 + CE_WEIGHT) * student_prob - teacher_prob - CE_WEIGHT * chosen.astype(jnp.float32))
    ).astype(jnp.bfloat16)
    hidden_grad = lax.psum_scatter(
        lax.dot_general(
            logit_grad, student_head, (((1,), (1,)), ((), ())), preferred_element_type=jnp.float32
        ),
        "vocab",
        scatter_dimension=1,
        tiled=True,
    )
    return (kl_loss, hidden_grad.astype(jnp.bfloat16))


def solution(mesh):
    placed = (
        P("rows", None),
        P(None, "vocab"),
        P("rows", "vocab"),
        P(None, "vocab"),
        P("rows"),
        P("rows"),
    )
    return jax.shard_map(
        local, mesh=mesh, in_specs=placed, out_specs=(P(), P("rows", "vocab")), check_vma=False
    )
```

profile of v0, /device:TPU:1, one launch (start us, length us, event | category | flops | bytes accessed | tf_op | source)
XLA Modules:
  0.0 884.7 jit_solution(12575870966822764194)
XLA Ops:
  7.2 0.0 all-gather.2.cloned.1.call-start
  7.2 0.7 all-gather.2.cloned.1.call-update
  7.9 0.0 reduce-scatter.2.cloned.1.call-start
  8.0 14.8 %fusion.19 = (f32[768]{0:T(1024)S(1)}, f32[768,1280]{1,0:T(8,128)}) fusion(bf16[768,4096]{1,0:T(8,128)(2,1)} %param.6, bf16[4096,1280]{1,0:T(8,128)(2,1)} %param.7), kind=kOutput, calls=%fused_computation.29 | convolution fusion | flops 8054045696 | bytes 20712448 | tf_op jit(solution)/shard_map/dot_general | solution.py:14
  22.7 0.0 copy-start.1
  22.7 98.6 %all-gather.2.cloned.1.call-done = bf16[768,3584]{0,1:T(8,128)(2,1)} async-done(((bf16[768,56]{0,1:T(8,128)(2,1)}), bf16[768,3584]{0,1:T(8,128)(2,1)}) %all-gather.2.cloned.1.call-update) | async-done | bytes 5505040 | tf_op jit(solution)/shard_map/all_gather | solution.py:15
  121.3 13.4 %fusion.18 = (f32[768]{0:T(1024)S(1)}, f32[768,1280]{1,0:T(8,128)}) fusion(bf16[768,3584]{0,1:T(8,128)(2,1)} %all-gather.2.cloned.1.call-done, bf16[3584,1280]{1,0:T(8,128)(2,1)} %param.9), kind=kOutput, calls=%fused_computation.28 | convolution fusion | flops 7047412736 | bytes 18615296 | tf_op jit(solution)/shard_map/dot_general | solution.py:16
  134.7 140.1 %all-reduce.1 = (f32[768]{0:T(1024)S(1)}, f32[768]{0:T(1024)S(1)}) all-reduce(f32[768]{0:T(1024)S(1)} %get-tuple-element.18, f32[768]{0:T(1024)S(1)} %get-tuple-element.20), channel_id=1, replica_groups=mesh['rows'=2,'vocab'=64] {'vocab'}, use_global_device_ids=true, to_apply=%region_7.8 | all-reduce | flops 1536 | bytes 12288 | tf_op jit(solution)/shard_map/pmax | solution.py:22
  274.8 0.0 copy-done.1
  274.8 0.0 copy-start
  274.9 4.5 multiply_reduce_fusion
  279.4 272.0 %all-reduce = (f32[768]{0:T(1024)S(1)}, f32[768]{0:T(1024)S(1)}, f32[768]{0:T(1024)S(1)}, f32[768]{0:T(1024)S(1)}) all-reduce(f32[768]{0:T(1024)S(1)} %get-tuple-element.5, f32[768]{0:T(1024)S(1)} %get-tuple-element.4, f32[768]{0:T(1024)S(1)} %get-tuple-element.3, ...), channel_id=1, replica_groups=mesh['rows'=2,'vocab'=64] {'vocab'}, use_global_device_ids=true, to_apply=%region_9.10 | all-reduce | flops 3072 | bytes 24576 | tf_op jit(solution)/shard_map/psum | solution.py:27
  551.4 0.0 copy-done
  551.4 0.6 convert_reduce_fusion
  552.0 6.1 all-reduce.2
  558.1 0.6 convert_divide_fusion
  558.7 15.4 %fusion.5 = f32[768,3584]{0,1:T(8,128)} fusion(bf16[3584,1280]{1,0:T(8,128)(2,1)} %param.9, f32[768,1280]{1,0:T(8,128)} %get-tuple-element.21, f32[768,1280]{1,0:T(8,128)} %get-tuple-element.19, f32[768]{0:T(1024)S(1)} %get-tuple-element.16, f32[768]{0:T(1024)S(1)} %get-tuple-element.17, f32[768]{0:T(1024)S(1)} %convert_divide_fusion, ...), kind=kOutput, calls=%fused_computation.10 | convolution fusion | flops 7055278080 | bytes 28066816 | tf_op jit(solution)/shard_map/dot_general | solution.py:50
  574.1 0.0 reduce-scatter.2.cloned.1.call-update
  575.5 299.7 %reduce-scatter.2.cloned.1.call-done = f32[768,56]{0,1:T(8,128)} async-done(((f32[768,3584]{0,1:T(8,128)}), f32[768,56]{0,1:T(8,128)}) %reduce-scatter.2.cloned.1.call-update) | async-done | bytes 172048 | tf_op jit(solution)/shard_map/reduce_scatter | solution.py:49
  875.2 1.6 convert_element_type.12
  (1 shorter events, 0.0 us)
Async XLA Ops:
  7.2 114.2 %all-gather.2.cloned.1.call-start = ((), (), s32[]{:S(2)}) async-start(), calls=%async_computation.1 | async-start | bytes 5591040 | tf_op jit(solution)/shard_map/all_gather | solution.py:15
  7.9 867.3 %reduce-scatter.2.cloned.1.call-start = ((), (), s32[]{:S(2)}) async-start(), calls=%async_computation.2 | async-start | bytes 11182080 | tf_op jit(solution)/shard_map/reduce_scatter | solution.py:49
  22.7 252.1 %copy-start.1 = (s32[768]{0:T(1024)S(1)}, s32[768]{0:T(1024)}, u32[]{:S(2)}) copy-start(s32[768]{0:T(1024)} %param.10) | copy-start | bytes 9220
  274.8 276.5 %copy-start = (s32[768]{0:T(1024)S(1)}, s32[768]{0:T(1024)}, u32[]{:S(2)}) copy-start(s32[768]{0:T(1024)} %param.11) | copy-start | bytes 9220
Sparse Core Ops, SparseCore 0:
  9.7 111.5 all-gather.1
  574.3 300.8 reduce-scatter.1
where the time goes:
time: 889 us; the launch traced here: 885 us
  blocking collectives  418 us (47%)
  waiting for transfers between devices  399 us (45%)
  matrix products  43.6 us (5%)
  between operations  16.6 us (2%)
    reduce_scatter x1, waiting for transfers between devices, local(): lax.psum_scatter(lax.dot_general(logit_grad, student_head, (((1,), (1,)),...  300 us
    psum x1, blocking collectives, local(): lax.psum((jnp.sum(t_exp, axis=1), jnp.sum(t_exp * difference, axis=1), jn...  272 us
    pmax x1, blocking collectives, local(): lax.pmax((jnp.max(teacher_logits, axis=1), jnp.max(student_logits, axis=1...  140 us
    all_gather x1, waiting for transfers between devices, local(): whole_hidden = lax.all_gather(student_hidden, 'vocab', axis=1, tiled=True)  98.6 us
  transfers between devices with their start and end apart: 2, of which 2 were waited for; matrix products, arithmetic and copies ran while one was open for 2% of the time, Pallas kernels for 0%

commit v1 on v0

v1 whole, which is shorter than its diff:
```python
import functools

import jax
import jax.numpy as jnp
from jax import lax
from jax.experimental import pallas as pl
from jax.experimental.pallas import tpu as pltpu
from jax.sharding import PartitionSpec as P

CE_WEIGHT = 0.5
F32, BF16 = jnp.float32, jnp.bfloat16
VMEM = pl.BlockSpec(memory_space=pltpu.VMEM)
ANY = pl.BlockSpec(memory_space=pl.ANY)
DMA = pltpu.SemaphoreType.DMA
LIMIT = 60 * 2**20


class Place:
    def __init__(self):
        v = lax.axis_index("vocab")
        self.x, self.z, self.y, self.c = v // 16, (v // 4) % 4, (v // 2) % 2, v % 2
        self.row = lax.axis_index("rows")

    def at(self, dx=0, dz=0, flip_y=False, flip_c=False):
        x, z = (self.x + dx) % 4, (self.z + dz) % 4
        y = 1 - self.y if flip_y else self.y
        c = 1 - self.c if flip_c else self.c
        return {"vocab": ((x * 4 + z) * 2 + y) * 2 + c}

    def peers(self):
        return (
            [self.at(dx=d) for d in (1, 2, 3)]
            + [self.at(dz=d) for d in (1, 2, 3)]
            + [self.at(flip_y=True), self.at(flip_c=True)]
        )

    def each_core(self, step):
        for core in (0, 1):
            pl.when(self.c == core)(functools.partial(step, core))

    def lead(self, core, d):
        return self.at(dx=d) if core == 0 else self.at(dz=d)

    def other(self, core, d):
        return self.at(dz=d) if core == 0 else self.at(dx=d)

    def own(self, core):
        return (self.x, self.z) if core == 0 else (self.z, self.x)


def piece(ref, prefix, core, p, q, y):
    x, z = (p, q) if core == 0 else (q, p)
    return ref.at[(*prefix, x, z, y)]


def send(src, dst, send_sem, recv_sem, device):
    return pltpu.make_async_remote_copy(
        src_ref=src,
        dst_ref=dst,
        send_sem=send_sem,
        recv_sem=recv_sem,
        device_id=device,
        device_id_type=pl.DeviceIdType.MESH,
    )


def greet(peers):
    barrier = pltpu.get_barrier_semaphore()
    for peer in peers:
        pl.semaphore_signal(barrier, inc=1, device_id=peer, device_id_type=pl.DeviceIdType.MESH)
    pl.semaphore_wait(barrier, len(peers))


ALL = slice(None)


class Gather:
    def __init__(self, place, ht, send_sem, recv_sem, relay_send, relay_recv):
        self.place, self.ht = place, ht
        self.sems = (send_sem, recv_sem)
        self.relay_sems = (relay_send, relay_recv)

    def slots(self, core, b):
        f, g = self.place.own(core)
        y = self.place.y
        s = (2 * b + core,)
        w = functools.partial(piece, self.ht, s, core)
        m = lambda i: i % 4
        return [
            w(f, g, 1 - y),
            w(m(f + 3), g, ALL),
            w(m(f + 2), g, ALL),
            w(m(f + 1), g, ALL),
            w(ALL, m(g + 3), ALL),
            w(ALL, m(g + 1), ALL),
            w(ALL, m(g + 2), 0),
            w(ALL, m(g + 2), 1),
        ]

    def copy(self, core, b, k):
        place = self.place
        f, g = place.own(core)
        w = functools.partial(piece, self.ht, (2 * b + core,), core)
        m = lambda i: i % 4
        src, device = [
            (w(f, g, place.y), place.at(flip_y=True)),
            (w(f, g, ALL), place.lead(core, 1)),
            (w(f, g, ALL), place.lead(core, 2)),
            (w(f, g, ALL), place.lead(core, 3)),
            (w(ALL, g, ALL), place.other(core, 1)),
            (w(ALL, g, ALL), place.other(core, 3)),
            (w(ALL, m(g + 3), 0), place.other(core, 1)),
            (w(ALL, m(g + 1), 1), place.other(core, 3)),
        ][k]
        return send(src, src, self.sems[0].at[b, k], self.sems[1].at[b, k], device)

    def relay(self, core, b, k):
        slot = self.slots(core, b)[k]
        return send(
            slot, slot, self.relay_sems[0].at[b, k], self.relay_sems[1].at[b, k], self.place.at(flip_c=True)
        )

    def start(self, b, ks):
        self.place.each_core(lambda core: [self.copy(core, b, k).start() for k in ks] and None)

    def arrive(self, b, ks, then=()):
        def step(core):
            slots = self.slots(core, b)
            for k in ks:
                send(slots[k], slots[k], self.sems[0].at[b, k], self.sems[1].at[b, k], self.place.at(flip_c=True)).wait_recv()
            for k in then:
                self.copy(core, b, k).start()
            for k in ks:
                self.relay(core, b, k).start()

        self.place.each_core(step)

    def relayed(self, b, ks=range(8)):
        def step(core):
            slots = self.slots(1 - core, b)
            for k in ks:
                send(
                    slots[k], slots[k], self.relay_sems[0].at[b, k], self.relay_sems[1].at[b, k], self.place.at(flip_c=True)
                ).wait_recv()

        self.place.each_core(step)

    def drain(self, b):
        def step(core):
            for k in range(8):
                self.copy(core, b, k).wait_send()
                self.relay(core, b, k).wait_send()

        self.place.each_core(step)


def forward_kernel(
    th_hbm, tw_hbm, hid, sw_hbm, t_out, s_out,
    th, tw, sw, ht, pair, local_sem, pair_sems, g_send, g_recv, r_send, r_recv,
):
    place = Place()
    loads = [pltpu.make_async_copy(th_hbm, th, local_sem.at[0])]
    tiles = tw.shape[0]
    for i in range(tiles):
        loads.append(pltpu.make_async_copy(tw_hbm.at[:, pl.ds(i * 256, 256)], tw.at[i], local_sem.at[1 + i]))
    loads.append(pltpu.make_async_copy(sw_hbm, sw, local_sem.at[1 + tiles]))
    for load in loads:
        load.start()
    greet(place.peers())
    swap = send(hid, pair, pair_sems.at[0], pair_sems.at[1], place.at(flip_c=True))
    swap.start()
    swap.wait()
    mine, theirs = hid[...].astype(F32), pair[...].astype(F32)
    first = place.c == 0
    both = jnp.concatenate([jnp.where(first, mine, theirs), jnp.where(first, theirs, mine)], axis=1)
    turned = both.T.astype(BF16)
    for s in range(6):
        ht[s, place.x, place.z, place.y] = turned[:, s * 128 : s * 128 + 128]
    gather = Gather(place, ht, g_send, g_recv, r_send, r_recv)
    for b in range(3):
        gather.start(b, [0])
    loads[0].wait()

    def tile(i, carry):
        pltpu.make_async_copy(tw_hbm.at[:, pl.ds(i * 256, 256)], tw.at[i], local_sem.at[1 + i]).wait()
        t_out[:, pl.ds(pl.multiple_of(i * 256, 256), 256)] = jnp.dot(th[...], tw[i], preferred_element_type=F32)

        @pl.when(i == 0)
        def _():
            lax.fori_loop(0, 3, lambda b, c: gather.arrive(b, [0], [1, 2, 3]), None)

        @pl.when(i == 1)
        def _():
            lax.fori_loop(0, 3, lambda b, c: gather.arrive(b, [1, 2, 3], [4, 5]), None)

        @pl.when(i == 3)
        def _():
            gather.arrive(0, [4, 5], [6, 7])

        @pl.when(i == 4)
        def _():
            gather.arrive(1, [4, 5], [6, 7])

        return carry

    lax.fori_loop(0, tiles, tile, None)
    loads[-1].wait()

    def block(b, carry):
        gather.arrive(b, [6, 7])
        gather.relayed(b)
        lhs = jnp.concatenate([ht[2 * b].reshape(3584, 128), ht[2 * b + 1].reshape(3584, 128)], axis=1)
        s_out[pl.ds(pl.multiple_of(b * 256, 256), 256), :] = lax.dot_general(
            lhs, sw[...], (((0,), (0,)), ((), ())), preferred_element_type=F32
        )

        @pl.when(b == 0)
        def _():
            gather.arrive(2, [4, 5], [6, 7])

        return carry

    lax.fori_loop(0, 3, block, None)
    lax.fori_loop(0, 3, lambda b, c: gather.drain(b), None)


def forward(th, tw, hid, sw):
    rows, cols = th.shape[0], tw.shape[1]
    out = jax.ShapeDtypeStruct((rows, cols), F32)
    return pl.pallas_call(
        forward_kernel,
        out_shape=(out, out),
        in_specs=[ANY, ANY, VMEM, ANY],
        out_specs=(VMEM, VMEM),
        scratch_shapes=[
            pltpu.VMEM(th.shape, BF16),
            pltpu.VMEM((cols // 256, th.shape[1], 256), BF16),
            pltpu.VMEM(sw.shape, BF16),
            pltpu.VMEM((6, 4, 4, 2, 112, 128), BF16),
            pltpu.VMEM(hid.shape, BF16),
            DMA((8,)),
            DMA((2,)),
            DMA((3, 8)),
            DMA((3, 8)),
            DMA((3, 8)),
            DMA((3, 8)),
        ],
        compiler_params=pltpu.CompilerParams(collective_id=0, has_side_effects=True, vmem_limit_bytes=LIMIT),
        name="forward",
    )(th, tw, hid, sw)


def merged(parts):
    t_max = functools.reduce(jnp.maximum, [p[0:1] for p in parts])
    s_max = functools.reduce(jnp.maximum, [p[3:4] for p in parts])
    t_w = [jnp.exp(p[0:1] - t_max) for p in parts]
    s_w = [jnp.exp(p[3:4] - s_max) for p in parts]
    t_sum = sum(w * p[1:2] for w, p in zip(t_w, parts))
    cross = sum(w * p[2:3] for w, p in zip(t_w, parts))
    s_sum = sum(w * p[4:5] for w, p in zip(s_w, parts))
    target = sum(p[5:6] for p in parts)
    return jnp.concatenate([t_max, t_sum, cross, s_max, s_sum, target, target, target], axis=0)


def stats_kernel(stats, mask, out, loss_out, hold, ex, ex_send, ex_recv, s_send, s_recv):
    place = Place()
    across = {"rows": 1 - place.row}
    greet(place.peers() + [across])
    weights = mask[...].astype(F32)
    ex[0] = jnp.broadcast_to(jnp.sum(weights, axis=1, keepdims=True), (8, 128))
    count = send(ex.at[0], ex.at[1], ex_send.at[0], ex_recv.at[0], across)
    count.start()

    def stage(k, base, size, index, devices):
        copies = [
            send(hold.at[base + index], hold.at[base + index], s_send.at[base + d], s_recv.at[base + d], devices[d - 1])
            for d in range(1, size)
        ]
        for copy in copies:
            copy.start()
        for d in range(1, size):
            slot = hold.at[base + (index + size - d) % size]
            send(slot, slot, s_send.at[base + d], s_recv.at[base + d], devices[d - 1]).wait_recv()
        total = merged([hold[base + i] for i in range(size)])
        return total, copies

    hold[place.c] = stats[...]
    total, sent0 = stage(0, 0, 2, place.c, [place.at(flip_c=True)])
    hold[2 + place.y] = total
    total, sent1 = stage(1, 2, 2, place.y, [place.at(flip_y=True)])
    hold[4 + place.x] = total
    total, sent2 = stage(2, 4, 4, place.x, [place.at(dx=d) for d in (1, 2, 3)])
    hold[8 + place.z] = total
    total, sent3 = stage(3, 8, 4, place.z, [place.at(dz=d) for d in (1, 2, 3)])
    for copy in sent0 + sent1 + sent2 + sent3:
        copy.wait_send()
    t_lse = total[0:1] + jnp.log(total[1:2])
    s_lse = total[3:4] + jnp.log(total[4:5])
    row_kl = total[2:3] / total[1:2] - t_lse + s_lse
    row_nll = s_lse - total[5:6]
    count.wait()
    masked = ex[0] + ex[1]
    part = jnp.sum(weights * (row_kl + CE_WEIGHT * row_nll), axis=1, keepdims=True)
    ex[2] = jnp.broadcast_to(part, (8, 128))
    loss = send(ex.at[2], ex.at[3], ex_send.at[1], ex_recv.at[1], across)
    loss.start()
    scale = weights / masked[0:1, 0:1]
    out[...] = jnp.concatenate([t_lse, s_lse, scale, scale, scale, scale, scale, scale], axis=0)
    loss.wait()
    loss_out[...] = (ex[2] + ex[3]) / masked


def reduce_stats(stats, mask):
    return pl.pallas_call(
        stats_kernel,
        out_shape=(jax.ShapeDtypeStruct(stats.shape, F32), jax.ShapeDtypeStruct((8, 128), F32)),
        in_specs=[VMEM, VMEM],
        out_specs=(VMEM, VMEM),
        scratch_shapes=[
            pltpu.VMEM((12,) + stats.shape, F32),
            pltpu.VMEM((4, 8, 128), F32),
            DMA((2,)),
            DMA((2,)),
            DMA((12,)),
            DMA((12,)),
        ],
        compiler_params=pltpu.CompilerParams(collective_id=1, has_side_effects=True),
        name="stats",
    )(stats, mask)


class Scatter:
    def __init__(self, place, pb, bufs, send_sem, recv_sem):
        self.place, self.pb = place, pb
        self.rp, self.ra, self.rb, self.mid, self.rc, self.cs, self.cf, self.ry, self.db = bufs
        self.ss, self.rs = send_sem, recv_sem

    def copies(self, core, b):
        return [functools.partial(self.copy, core, b, k) for k in range(10)]

    def copy(self, core, b, k):
        place = self.place
        f, g = place.own(core)
        y, c = place.y, core
        m = lambda i: i % 4
        w = functools.partial(piece, self.pb, (b, c), core)
        out = [
            (self.pb.at[b, 1 - c], self.rp.at[b], place.at(flip_c=True)),
            (w(m(f + 2), ALL, 0), self.ra.at[b, 0], place.lead(core, 1)),
            (w(m(f + 2), ALL, 1), self.ra.at[b, 1], place.lead(core, 3)),
            (w(m(f + 1), ALL, ALL), self.rb.at[b, 0], place.lead(core, 1)),
            (w(m(f + 3), ALL, ALL), self.rb.at[b, 1], place.lead(core, 3)),
            (self.mid.at[b, m(g + 1)], self.rc.at[b, 0], place.other(core, 1)),
            (self.mid.at[b, m(g + 2)], self.rc.at[b, 1], place.other(core, 2)),
            (self.mid.at[b, m(g + 3)], self.rc.at[b, 2], place.other(core, 3)),
            (self.cs.at[b], self.ry.at[b], place.at(flip_y=True)),
            (self.db.at[b, c], self.db.at[b, c], place.at(flip_c=True)),
        ]
        src, dst, device = out[k]
        return send(src, dst, self.ss.at[b, k], self.rs.at[b, k], device)

    def start_pair(self, b):
        self.place.each_core(lambda core: self.copy(core, b, 0).start())

    def lead_far(self, b):
        def step(core):
            copies = self.copies(core, b)
            copies[0]().wait_recv()
            self.pb[b, core] = (self.pb[b, core].astype(F32) + self.rp[b].astype(F32)).astype(BF16)
            copies[1]().start()
            copies[2]().start()

        self.place.each_core(step)

    def lead_near(self, b):
        def step(core):
            copies = self.copies(core, b)
            f, g = self.place.own(core)
            for k, step_to, y in ((1, 1, 0), (2, 3, 1)):
                copies[k]().wait_recv()
                at = piece(self.pb, (b, core), core, (f + step_to) % 4, ALL, y)
                at[...] = (at[...].astype(F32) + self.ra[b, k - 1].astype(F32)).astype(BF16)
                copies[k + 2]().start()

        self.place.each_core(step)

    def second(self, b):
        def step(core):
            copies = self.copies(core, b)
            f, g = self.place.own(core)
            copies[3]().wait_recv()
            copies[4]().wait_recv()
            mine = piece(self.pb, (b, core), core, f, ALL, ALL)
            self.mid[b] = (
                mine[...].astype(F32) + self.rb[b, 0].astype(F32) + self.rb[b, 1].astype(F32)
            ).astype(BF16)
            for k in (5, 6, 7):
                copies[k]().start()

        self.place.each_core(step)

    def third(self, b):
        def step(core):
            copies = self.copies(core, b)
            f, g = self.place.own(core)
            for k in (5, 6, 7):
                copies[k]().wait_recv()
            total = self.mid.at[b, g][...].astype(F32)
            for d in range(3):
                total = total + self.rc[b, d].astype(F32)
            first = self.place.y == 0
            self.cf[b] = jnp.where(first, total[0], total[1])
            self.cs[b] = jnp.where(first, total[1], total[0]).astype(BF16)
            copies[8]().start()

        self.place.each_core(step)

    def last(self, b):
        def step(core):
            copies = self.copies(core, b)
            copies[8]().wait_recv()
            self.db[b, core] = (self.cf[b] + self.ry[b].astype(F32)).astype(BF16)
            copies[9]().start()

        self.place.each_core(step)

    def finish(self, b, out):
        def step(core):
            copies = self.copies(core, b)
            slot = self.db.at[b, 1 - core]
            send(slot, slot, self.ss.at[b, 9], self.rs.at[b, 9], self.place.at(flip_c=True)).wait_recv()
            for k, copy in enumerate(copies):
                copy().wait_send()
            whole = jnp.concatenate([self.db[b, 0].astype(F32), self.db[b, 1].astype(F32)], axis=1)
            mine = whole[core * 56 : core * 56 + 56]
            out[pl.ds(pl.multiple_of(b * 256, 256), 256), :] = mine.T.astype(BF16)

        self.place.each_core(step)


def backward_kernel(grad, sw, out, pb, rp, ra, rb, mid, rc, cs, cf, ry, db, s_send, s_recv):
    place = Place()
    greet(place.peers())
    scatter = Scatter(place, pb, (rp, ra, rb, mid, rc, cs, cf, ry, db), s_send, s_recv)

    def block(b, carry):
        rows = grad[pl.ds(pl.multiple_of(b * 256, 256), 256), :]

        def chunk(i, carry):
            part = lax.dot_general(
                sw[pl.ds(pl.multiple_of(i * 896, 896), 896), :],
                rows,
                (((1,), (1,)), ((), ())),
                preferred_element_type=F32,
            ).astype(BF16)
            pb[b, 0, i] = part[:, :128].reshape(4, 2, 112, 128)
            pb[b, 1, i] = part[:, 128:].reshape(4, 2, 112, 128)
            return carry

        lax.fori_loop(0, 4, chunk, None)
        scatter.start_pair(b)

        @pl.when(b > 0)
        def _():
            scatter.lead_far(b - 1)

        @pl.when(b > 1)
        def _():
            scatter.lead_near(b - 2)

        return carry

    lax.fori_loop(0, 3, block, None)
    scatter.lead_far(2)
    scatter.lead_near(1)
    scatter.second(0)
    scatter.lead_near(2)
    scatter.second(1)
    scatter.third(0)
    scatter.second(2)
    scatter.third(1)
    scatter.last(0)
    scatter.third(2)
    scatter.last(1)
    scatter.finish(0, out)
    scatter.last(2)
    scatter.finish(1, out)
    scatter.finish(2, out)


def backward(grad, sw):
    rows = grad.shape[0]
    return pl.pallas_call(
        backward_kernel,
        out_shape=jax.ShapeDtypeStruct((rows, 56), BF16),
        in_specs=[VMEM, VMEM],
        out_specs=VMEM,
        scratch_shapes=[
            pltpu.VMEM((3, 2, 4, 4, 2, 112, 128), BF16),
            pltpu.VMEM((3, 4, 4, 2, 112, 128), BF16),
            pltpu.VMEM((3, 2, 4, 112, 128), BF16),
            pltpu.VMEM((3, 2, 4, 2, 112, 128), BF16),
            pltpu.VMEM((3, 4, 2, 112, 128), BF16),
            pltpu.VMEM((3, 3, 2, 112, 128), BF16),
            pltpu.VMEM((3, 112, 128), BF16),
            pltpu.VMEM((3, 112, 128), F32),
            pltpu.VMEM((3, 112, 128), BF16),
            pltpu.VMEM((3, 2, 112, 128), BF16),
            DMA((3, 10)),
            DMA((3, 10)),
        ],
        compiler_params=pltpu.CompilerParams(collective_id=2, has_side_effects=True, vmem_limit_bytes=LIMIT),
        name="backward",
    )(grad, sw)


def local(teacher_hidden, teacher_head, student_hidden, student_head, token_ids, response_mask):
    shard_cols = teacher_head.shape[1]
    row_count = teacher_hidden.shape[0]
    t_logits, s_logits = forward(teacher_hidden, teacher_head, student_hidden, student_head)
    first_col = lax.axis_index("vocab") * shard_cols
    columns = first_col + lax.broadcasted_iota(jnp.int32, (row_count, shard_cols), 1)
    chosen = columns == token_ids[:, None]
    t_max, s_max = jnp.max(t_logits, axis=1), jnp.max(s_logits, axis=1)
    t_exp = jnp.exp(t_logits - t_max[:, None])
    s_exp = jnp.exp(s_logits - s_max[:, None])
    target = jnp.sum(jnp.where(chosen, s_logits, 0.0), axis=1)
    stats = jnp.stack(
        [
            t_max,
            jnp.sum(t_exp, axis=1),
            jnp.sum(t_exp * (t_logits - s_logits), axis=1),
            s_max,
            jnp.sum(s_exp, axis=1),
            target,
            target,
            target,
        ]
    )
    final, loss = reduce_stats(stats, response_mask[None, :])
    teacher_prob = jnp.exp(t_logits - final[0][:, None])
    student_prob = jnp.exp(s_logits - final[1][:, None])
    logit_grad = (
        final[2][:, None]
        * ((1.0 + CE_WEIGHT) * student_prob - teacher_prob - CE_WEIGHT * chosen.astype(F32))
    ).astype(BF16)
    return loss[0, 0], backward(logit_grad, student_head)


def solution(mesh):
    placed = (
        P("rows", None),
        P(None, "vocab"),
        P("rows", "vocab"),
        P(None, "vocab"),
        P("rows"),
        P("rows"),
    )
    return jax.shard_map(
        local, mesh=mesh, in_specs=placed, out_specs=(P(), P("rows", "vocab")), check_vma=False
    )
```

time: 889 us -> 129 us (0.15)
  blocking collectives: 418 us -> 0 us
  waiting for transfers between devices: 399 us -> 0 us
  Pallas kernels: 0 us -> 105 us
  matrix products: 43.6 us -> 0 us
  between operations: 16.6 us -> 0.74 us
    reduce_scatter x1 -> x0, waiting for transfers between devices: 300 us -> none  [local(): lax.psum_scatter(lax.dot_general(logit_grad, student_head, (((1,), (1,)),...]
    psum x2 -> x0, blocking collectives: 278 us -> none  [the longest x1 272 us: local(): lax.psum((jnp.sum(t_exp, axis=1), jnp.sum(t_exp * difference, axis=1), jn...]
    pmax x1 -> x0, blocking collectives: 140 us -> none  [local(): lax.pmax((jnp.max(teacher_logits, axis=1), jnp.max(student_logits, axis=1...]
    pallas_call x0 -> x3, Pallas kernels: none -> 105 us  [the longest x1 44.8 us: forward(): pl.pallas_call(forward_kernel, out_shape=(out, out), in_specs=[ANY, ANY,...]
    all_gather x1 -> x0, waiting for transfers between devices: 98.6 us -> none  [local(): whole_hidden = lax.all_gather(student_hidden, 'vocab', axis=1, tiled=True)]
    dot_general x3 -> x0, matrix products: 43.6 us -> none  [the longest x1 15.4 us: local(): lax.dot_general(logit_grad, student_head, (((1,), (1,)), ((), ())), prefe...]
  transfers between devices with their start and end apart: 2 -> 0, of which waited for: 2 -> 0; matrix products, arithmetic and copies ran while one was open for 2% -> 0% of each run, Pallas kernels for 0% -> 0%
where the time goes in v1:
time: 129 us; the launch traced here: 128 us
  Pallas kernels  105 us (81%)
  other arithmetic  14.5 us (11%)
  local copies, waits for them, and re-layouts  7.41 us (6%)
    pallas_call x1, Pallas kernels, forward(): pl.pallas_call(forward_kernel, out_shape=(out, out), in_specs=[ANY, ANY,...  44.8 us
    pallas_call x1, Pallas kernels, backward(): pl.pallas_call(backward_kernel, out_shape=jax.ShapeDtypeStruct((rows, 56)...  44.8 us
    pallas_call x1, Pallas kernels, reduce_stats(): pl.pallas_call(stats_kernel, out_shape=(jax.ShapeDtypeStruct(stats.shape,...  15.9 us
    convert_element_type x1, other arithmetic, local(): logit_grad = (final[2][:, None] * ((1.0 + CE_WEIGHT) * student_prob - tea...  5.3 us
    reduce_max x2, other arithmetic, local(): t_max, s_max = (jnp.max(t_logits, axis=1), jnp.max(s_logits, axis=1))  4.74 us
    reduce_sum x1, other arithmetic, local(): target = jnp.sum(jnp.where(chosen, s_logits, 0.0), axis=1)  4.47 us
    unnamed x4, local copies, waits for them, and re-layouts  3.39 us

profile of v1, /device:TPU:1, one launch (start us, length us, event | category | flops | bytes accessed | tf_op | source)
XLA Modules:
  0.0 128.1 jit_solution(10636320305883498464)
XLA Ops:
  0.6 1.3 %broadcast_in_dim.11.mask = s32[1,768]{1,0:T(1,128)} reshape(s32[768]{0:T(1024)} %param.11) | data formatting | bytes 6144 | tf_op jit(solution)/shard_map/broadcast_in_dim | solution.py:540
  1.9 1.7 %copy.8.hid = bf16[768,56]{1,0:T(8,128)(2,1)} copy(bf16[768,56]{0,1:T(8,128)(2,1)} %param.8) | data formatting | bytes 172032 | tf_op args[2]
  3.6 44.8 %forward.1 = (f32[768,1280]{1,0:T(8,128)}, f32[768,1280]{1,0:T(8,128)}) custom-call(bf16[768,4096]{1,0:T(8,128)(2,1)} %th_hbm.1, bf16[4096,1280]{1,0:T(8,128)(2,1)} %tw_hbm.1, bf16[768,56]{1,0:T(8,128)(2,1)} %copy.8.hid, bf16[3584,1280]{1,0:T(8,128)(2,1)} %sw.1), custom_call_target="tpu_custom_call" | custom-call | tf_op jit(solution)/shard_map/forward/pallas_call | solution.py:230
  48.4 0.0 copy-start
  48.4 2.4 %reduce_max.18 = f32[768]{0:T(1024)S(1)} reduce(f32[768,1280]{1,0:T(8,128)} %get-tuple-element.6, f32[]{:T(128)} %constant.6.clone.1), dimensions={1}, to_apply=%region_0.0 | reduce | flops 982272 | bytes 3935236 | tf_op jit(solution)/shard_map/reduce_max | solution.py:524
  50.8 2.4 %reduce_max.19 = f32[768]{0:T(1024)S(1)} reduce(f32[768,1280]{1,0:T(8,128)} %get-tuple-element.7, f32[]{:T(128)} %constant.6.clone.1), dimensions={1}, to_apply=%region_3.4 | reduce | flops 982272 | bytes 3935236 | tf_op jit(solution)/shard_map/reduce_max | solution.py:524
  53.2 0.0 copy-done
  53.2 4.5 %fusion = (f32[768]{0:T(1024)S(1)}, f32[768]{0:T(1024)S(1)}, f32[768]{0:T(1024)S(1)}, f32[768]{0:T(1024)S(1)}) fusion(f32[768,1280]{1,0:T(8,128)} %get-tuple-element.7, s32[1280]{0:T(1024)S(1)} %iota_add_fusion, s32[768]{0:T(1024)S(1)} %copy-done, f32[768]{0:T(1024)S(1)} %reduce_max.19, f32[768,1280]{1,0:T(8,128)} %get-tuple-element.6, f32[768]{0:T(1024)S(1)} %reduce_max.18), kind=kLoop, calls=%fused_computation.2 | loop fusion | flops 9827328 | bytes 7890944 | tf_op jit(solution)/shard_map/reduce_sum | solution.py:527
  57.7 0.7 stack.29.stats
  58.4 15.9 %stats.1 = (f32[8,768]{1,0:T(8,128)}, f32[8,128]{1,0:T(8,128)}) custom-call(f32[8,768]{1,0:T(8,128)} %stack.29.stats, s32[1,768]{1,0:T(1,128)} %broadcast_in_dim.11.mask), custom_call_target="tpu_custom_call" | custom-call | tf_op jit(solution)/shard_map/stats/pallas_call | solution.py:314
  74.2 1.2 slice.12
  75.4 0.9 slice_reduce_fusion.2
  76.3 5.3 %fusion.3.grad = bf16[768,1280]{1,0:T(8,128)(2,1)} fusion(f32[768,1280]{1,0:T(8,128)} %get-tuple-element.6, f32[768,1280]{1,0:T(8,128)} %get-tuple-element.7, f32[768]{0:T(1024)S(1)} %get-tuple-element.19, f32[768]{0:T(1024)S(1)} %get-tuple-element.20, f32[768]{0:T(1024)S(1)} %get-tuple-element.18, s32[1280]{0:T(1024)S(1)} %iota_add_fusion, s32[768]{0:T(1024)S(1)} %copy-done), kind=kLoop, calls=%fused_computation.5 | loop fusion | flops 8847360 | bytes 9847808 | tf_op jit(solution)/shard_map/convert_element_type | solution.py:546
  81.6 44.8 %backward.1 = bf16[768,56]{1,0:T(8,128)(2,1)} custom-call(bf16[768,1280]{1,0:T(8,128)(2,1)} %fusion.3.grad, bf16[3584,1280]{1,0:T(8,128)(2,1)} %sw.1), custom_call_target="tpu_custom_call" | custom-call | tf_op jit(solution)/shard_map/backward/pallas_call | solution.py:493
  126.4 1.7 %copy.9 = bf16[768,56]{0,1:T(8,128)(2,1)} copy(bf16[768,56]{1,0:T(8,128)(2,1)} %backward.1) | data formatting | bytes 172032
  (7 shorter events, 0.0 us)
Async XLA Ops:
  48.4 4.8 %copy-start = (s32[768]{0:T(1024)S(1)}, s32[768]{0:T(1024)}, u32[]{:S(2)}) copy-start(s32[768]{0:T(1024)} %param.10) | copy-start | bytes 9220

commit v2 on v0

v2 whole, which is shorter than its diff:
```python
import functools

import jax
import jax.numpy as jnp
from jax import lax
from jax.experimental import pallas as pl
from jax.experimental.pallas import tpu as pltpu
from jax.sharding import PartitionSpec as P

CE_WEIGHT = 0.5
F32, BF16 = jnp.float32, jnp.bfloat16
VMEM = pl.BlockSpec(memory_space=pltpu.VMEM)
ANY = pl.BlockSpec(memory_space=pl.ANY)
DMA = pltpu.SemaphoreType.DMA
LIMIT = 60 * 2**20


class Place:
    def __init__(self):
        v = lax.axis_index("vocab")
        self.x, self.z, self.y, self.c = v // 16, (v // 4) % 4, (v // 2) % 2, v % 2
        self.row = lax.axis_index("rows")

    def at(self, dx=0, dz=0, flip_y=False, flip_c=False):
        x, z = (self.x + dx) % 4, (self.z + dz) % 4
        y = 1 - self.y if flip_y else self.y
        c = 1 - self.c if flip_c else self.c
        return {"vocab": ((x * 4 + z) * 2 + y) * 2 + c}

    def peers(self):
        return (
            [self.at(dx=d, flip_y=f) for d in (1, 2, 3) for f in (False, True)]
            + [self.at(dz=d, flip_y=f) for d in (1, 2, 3) for f in (False, True)]
            + [self.at(dx=d, flip_c=True) for d in (1, 2, 3)]
            + [self.at(flip_y=True), self.at(flip_c=True)]
        )

    def each_core(self, step):
        for core in (0, 1):
            pl.when(self.c == core)(functools.partial(step, core))

    def lead(self, core, d, flip=False):
        return self.at(dx=d, flip_y=flip) if core == 0 else self.at(dz=d, flip_y=flip)

    def other(self, core, d, flip=False):
        return self.lead(1 - core, d, flip)

    def own(self, core):
        return (self.x, self.z) if core == 0 else (self.z, self.x)


def piece(ref, prefix, core, p, q, y):
    x, z = (p, q) if core == 0 else (q, p)
    return ref.at[(*prefix, x, z, y)]


def send(src, dst, send_sem, recv_sem, device):
    return pltpu.make_async_remote_copy(
        src_ref=src,
        dst_ref=dst,
        send_sem=send_sem,
        recv_sem=recv_sem,
        device_id=device,
        device_id_type=pl.DeviceIdType.MESH,
    )


ALL = slice(None)


SEVEN = ((1, False), (3, False), (0, True), (1, True), (3, True), (2, False), (2, True))


class Gather:
    def __init__(self, place, ht, send_sem, recv_sem, relay_send, relay_recv):
        self.place, self.ht = place, ht
        self.ss, self.rs, self.relay_ss, self.relay_rs = send_sem, recv_sem, relay_send, relay_recv

    def copy(self, core, b, k):
        place = self.place
        f, g = place.own(core)
        w = functools.partial(piece, self.ht, (2 * b + core,), core)
        if k < 7:
            d, flip = SEVEN[k]
            src, device = w(f, g, place.y), place.lead(core, d, flip)
        else:
            src, device = [
                (w(ALL, g, ALL), place.other(core, 1)),
                (w(ALL, g, ALL), place.other(core, 3)),
                (w(ALL, (g + 3) % 4, 0), place.other(core, 1)),
                (w(ALL, (g + 1) % 4, 1), place.other(core, 3)),
            ][k - 7]
        return send(src, src, self.ss.at[b, k], self.rs.at[b, k], device)

    def landed(self, core, b, k):
        f, g = self.place.own(core)
        w = functools.partial(piece, self.ht, (2 * b + core,), core)
        if k < 7:
            d, flip = SEVEN[k]
            slot = w((f + 4 - d) % 4, g, 1 - self.place.y if flip else self.place.y)
        else:
            slot = [w(ALL, (g + 3) % 4, ALL), w(ALL, (g + 1) % 4, ALL), w(ALL, (g + 2) % 4, 0), w(ALL, (g + 2) % 4, 1)][k - 7]
        send(slot, slot, self.ss.at[b, k], self.rs.at[b, k], self.place.at(flip_c=True)).wait_recv()

    def relay(self, core, b, k):
        f, g = self.place.own(core)
        w = functools.partial(piece, self.ht, (2 * b + core,), core)
        slot = [
            w(ALL, g, ALL),
            w(ALL, (g + 3) % 4, ALL),
            w(ALL, (g + 1) % 4, ALL),
            w(ALL, (g + 2) % 4, 0),
            w(ALL, (g + 2) % 4, 1),
        ][k]
        return send(slot, slot, self.relay_ss.at[b, k], self.relay_rs.at[b, k], self.place.at(flip_c=True))

    def first(self, b):
        def step(core):
            for k in range(7):
                self.copy(core, b, k).start()

        self.place.each_core(step)

    def plane(self, b):
        def step(core):
            for k in range(7):
                self.landed(core, b, k)
            self.copy(core, b, 7).start()
            self.copy(core, b, 8).start()
            self.relay(core, b, 0).start()

        self.place.each_core(step)

    def onward(self, b):
        def step(core):
            for k in (7, 8):
                self.landed(core, b, k)
                self.copy(core, b, k + 2).start()
                self.relay(core, b, k - 6).start()

        self.place.each_core(step)

    def whole(self, b):
        def step(core):
            for k in (9, 10):
                self.landed(core, b, k)
                self.relay(core, b, k - 6).start()
            for k in range(5):
                self.relay(1 - core, b, k).wait_recv()

        self.place.each_core(step)

    def drain(self, b):
        def step(core):
            for k in range(11):
                self.copy(core, b, k).wait_send()
            for k in range(5):
                self.relay(core, b, k).wait_send()

        self.place.each_core(step)


def merged(parts):
    t_max = functools.reduce(jnp.maximum, [p[0:1] for p in parts])
    s_max = functools.reduce(jnp.maximum, [p[3:4] for p in parts])
    t_w = [jnp.exp(p[0:1] - t_max) for p in parts]
    s_w = [jnp.exp(p[3:4] - s_max) for p in parts]
    t_sum = sum(w * p[1:2] for w, p in zip(t_w, parts))
    cross = sum(w * p[2:3] for w, p in zip(t_w, parts))
    s_sum = sum(w * p[4:5] for w, p in zip(s_w, parts))
    target = sum(p[5:6] for p in parts)
    return jnp.concatenate([t_max, t_sum, cross, s_max, s_sum, target, target, target], axis=0)


class Statistics:
    def __init__(self, place, hold, send_sem, recv_sem):
        self.place, self.hold, self.ss, self.rs = place, hold, send_sem, recv_sem

    def copies(self, b, stage):
        place = self.place
        own = self.own(stage)
        out = []
        for k, (d, flip) in enumerate(SEVEN):
            device = place.at(dx=d, flip_c=flip) if stage == 0 else place.at(dz=d, flip_y=flip)
            slot = self.hold.at[b, stage, own]
            out.append(send(slot, slot, self.ss.at[b, stage, k], self.rs.at[b, stage, k], device))
        return out

    def own(self, stage):
        place = self.place
        return place.x * 2 + place.c if stage == 0 else place.z * 2 + place.y

    def start(self, b, stage, value):
        self.hold[b, stage, self.own(stage)] = value
        for copy in self.copies(b, stage):
            copy.start()

    def total(self, b, stage):
        place = self.place
        main, pair = (place.x, place.c) if stage == 0 else (place.z, place.y)
        for k, (d, flip) in enumerate(SEVEN):
            index = (main + 4 - d) % 4 * 2 + (1 - pair if flip else pair)
            slot = self.hold.at[b, stage, index]
            send(slot, slot, self.ss.at[b, stage, k], self.rs.at[b, stage, k], place.at(flip_c=True)).wait_recv()
        return merged([self.hold[b, stage, i] for i in range(8)])

    def drain(self, b):
        for stage in (0, 1):
            for copy in self.copies(b, stage):
                copy.wait_send()


class Scatter:
    def __init__(self, place, pb, bufs, send_sem, recv_sem):
        self.place, self.pb = place, pb
        self.rp, self.ra, self.rb, self.mid, self.rc, self.db = bufs
        self.ss, self.rs = send_sem, recv_sem

    def copy(self, core, b, k):
        place = self.place
        f, g = place.own(core)
        w = functools.partial(piece, self.pb, (b, core), core)
        if 5 <= k < 12:
            d, flip = SEVEN[k - 5]
            src = self.mid.at[b, (g + d) % 4, 1 - place.y if flip else place.y]
            dst, device = self.rc.at[b, k - 5], place.other(core, d, flip)
        else:
            src, dst, device = {
                0: lambda: (self.pb.at[b, 1 - core], self.rp.at[b], place.at(flip_c=True)),
                1: lambda: (w((f + 2) % 4, ALL, 0), self.ra.at[b, 0], place.lead(core, 1)),
                2: lambda: (w((f + 2) % 4, ALL, 1), self.ra.at[b, 1], place.lead(core, 3)),
                3: lambda: (w((f + 1) % 4, ALL, ALL), self.rb.at[b, 0], place.lead(core, 1)),
                4: lambda: (w((f + 3) % 4, ALL, ALL), self.rb.at[b, 1], place.lead(core, 3)),
                12: lambda: (self.db.at[b, core], self.db.at[b, core], place.at(flip_c=True)),
            }[k]()
        return send(src, dst, self.ss.at[b, k], self.rs.at[b, k], device)

    def start_pair(self, b):
        self.place.each_core(lambda core: self.copy(core, b, 0).start())

    def lead_far(self, b):
        def step(core):
            self.copy(core, b, 0).wait_recv()
            self.pb[b, core] = (self.pb[b, core].astype(F32) + self.rp[b].astype(F32)).astype(BF16)
            self.copy(core, b, 1).start()
            self.copy(core, b, 2).start()

        self.place.each_core(step)

    def lead_near(self, b):
        def step(core):
            f, g = self.place.own(core)
            for k, ahead, y in ((1, 1, 0), (2, 3, 1)):
                self.copy(core, b, k).wait_recv()
                at = piece(self.pb, (b, core), core, (f + ahead) % 4, ALL, y)
                at[...] = (at[...].astype(F32) + self.ra[b, k - 1].astype(F32)).astype(BF16)
                self.copy(core, b, k + 2).start()

        self.place.each_core(step)

    def second(self, b):
        def step(core):
            f, g = self.place.own(core)
            self.copy(core, b, 3).wait_recv()
            self.copy(core, b, 4).wait_recv()
            mine = piece(self.pb, (b, core), core, f, ALL, ALL)
            self.mid[b] = (mine[...].astype(F32) + self.rb[b, 0].astype(F32) + self.rb[b, 1].astype(F32)).astype(BF16)
            for k in range(5, 12):
                self.copy(core, b, k).start()

        self.place.each_core(step)

    def last(self, b):
        def step(core):
            f, g = self.place.own(core)
            for k in range(5, 12):
                self.copy(core, b, k).wait_recv()
            total = self.mid.at[b, g, self.place.y][...].astype(F32)
            for k in range(7):
                total = total + self.rc[b, k].astype(F32)
            self.db[b, core] = total.astype(BF16)
            self.copy(core, b, 12).start()

        self.place.each_core(step)

    def finish(self, b, out):
        def step(core):
            slot = self.db.at[b, 1 - core]
            send(slot, slot, self.ss.at[b, 12], self.rs.at[b, 12], self.place.at(flip_c=True)).wait_recv()
            for k in range(13):
                self.copy(core, b, k).wait_send()
            for half in (0, 1):
                mine = self.db[b, half].astype(F32)[core * 56 : core * 56 + 56]
                out[:, b * 256 + half * 128 : b * 256 + half * 128 + 128] = mine.astype(BF16)

        self.place.each_core(step)


def kernel(
    th_hbm, tw_hbm, hid, sw_hbm, tok, mask, loss_out, out,
    th, tw, sw, ht, pair, et, es, gb, info, tcol, col, coef, hold, ex, lossv, pb, rp, ra, rb, mid, rc, db,
    local_sem, pair_sems, ex_send, ex_recv, g_send, g_recv, r_send, r_recv, st_send, st_recv, s_send, s_recv,
):
    place = Place()
    across = {"rows": 1 - place.row}
    peers = place.peers() + [across]
    barrier = pltpu.get_barrier_semaphore()
    for peer in peers:
        pl.semaphore_signal(barrier, inc=1, device_id=peer, device_id_type=pl.DeviceIdType.MESH)

    th_load = lambda i: pltpu.make_async_copy(th_hbm.at[pl.ds(i * 128, 128)], th.at[pl.ds(i * 128, 128)], local_sem.at[i])
    tw_load = lambda i: pltpu.make_async_copy(
        tw_hbm.at[pl.ds(i * 1024, 1024)], tw.at[pl.ds(i * 1024, 1024)], local_sem.at[6 + i]
    )
    sw_load = lambda i: pltpu.make_async_copy(
        sw_hbm.at[pl.ds(i * 896, 896)], sw.at[pl.ds(i * 896, 896)], local_sem.at[10 + i]
    )
    th_load(0).start()
    for i in range(4):
        tw_load(i).start()
    for i in range(1, 6):
        th_load(i).start()
    for i in range(4):
        sw_load(i).start()

    mine = jnp.concatenate([hid[...].astype(F32), jnp.zeros((8, 768), F32)], axis=0).astype(BF16)
    for b in range(3):
        for half in (0, 1):
            pair[0, b, half] = mine[:, b * 256 + half * 128 : b * 256 + half * 128 + 128]
    pl.semaphore_wait(barrier, len(peers))
    swaps = [
        send(
            pair.at[0, b, 1 - place.c], pair.at[1, b, 1 - place.c], pair_sems.at[0, b], pair_sems.at[1, b], place.at(flip_c=True)
        )
        for b in range(3)
    ]
    for swap in swaps:
        swap.start()

    weights = mask[...].astype(F32).reshape(1, 768)
    ex[0] = jnp.broadcast_to(jnp.sum(weights, axis=1, keepdims=True), (8, 128))
    count = send(ex.at[0], ex.at[1], ex_send.at[0], ex_recv.at[0], across)
    count.start()
    gather = Gather(place, ht, g_send, g_recv, r_send, r_recv)

    for b in range(3):
        slot = pair.at[1, b, place.c]
        send(slot, slot, pair_sems.at[0, b], pair_sems.at[1, b], place.at(flip_c=True)).wait_recv()
        own = pair[0, b, place.c].astype(F32)[:56]
        theirs = pair[1, b, place.c].astype(F32)[:56]
        first = place.c == 0
        both = jnp.concatenate([jnp.where(first, own, theirs), jnp.where(first, theirs, own)], axis=0)
        ht[2 * b + place.c, place.x, place.z, place.y] = both.astype(BF16)
        gather.first(b)

    first_col = lax.axis_index("vocab") * 1280
    local_tok = (tok[...] - first_col).astype(F32).reshape(1, 768)
    info[...] = jnp.broadcast_to(local_tok, (128, 768)).T

    for i in range(4):
        tw_load(i).wait()

    def teacher(i, carry):
        rows = pl.ds(pl.multiple_of(i * 128, 128), 128)
        th_load(i).wait()
        et[rows, :] = jnp.dot(th[rows, :], tw[...], preferred_element_type=F32)
        pl.when(i == 2)(lambda: gather.plane(0))
        pl.when(i == 3)(lambda: gather.plane(1))
        pl.when(i == 4)(lambda: gather.plane(2))
        pl.when(i == 5)(lambda: gather.onward(0))
        return carry

    lax.fori_loop(0, 6, teacher, None)

    lane = lax.broadcasted_iota(jnp.int32, (32, 128), 1)

    def teacher_rows(i, carry):
        rows = pl.ds(pl.multiple_of(i * 32, 32), 32)
        t = et[rows, :]
        top = jnp.max(t, axis=1, keepdims=True)
        e = jnp.exp(t - top)
        et[rows, :] = e
        total = jnp.sum(e, axis=1, keepdims=True)
        mean = jnp.sum(e * t, axis=1, keepdims=True)
        tcol[rows, :] = jnp.where(lane == 0, top, jnp.where(lane == 1, total, jnp.where(lane == 2, mean, 0.0)))
        return carry

    lax.fori_loop(0, 12, teacher_rows, None)
    gather.onward(1)
    lax.fori_loop(12, 24, teacher_rows, None)
    gather.onward(2)
    for i in range(4):
        sw_load(i).wait()
    count.wait()

    stats = Statistics(place, hold, st_send, st_recv)
    column = lax.broadcasted_iota(jnp.int32, (32, 1280), 1).astype(F32)

    def student_rows(b):
        def step(i, carry):
            rows = pl.ds(pl.multiple_of(b * 256 + i * 32, 32), 32)
            s = es[rows, :]
            top = jnp.max(s, axis=1, keepdims=True)
            e = jnp.exp(s - top)
            es[rows, :] = e
            total = jnp.sum(e, axis=1, keepdims=True)
            mean = jnp.sum(et[rows, :] * s, axis=1, keepdims=True)
            target = jnp.sum(jnp.where(column == info[rows, 0:1], s, 0.0), axis=1, keepdims=True)
            old = tcol[rows, :]
            new = jnp.where(lane == 2, old - mean, old)
            new = jnp.where(lane == 3, top, jnp.where(lane == 4, total, jnp.where(lane == 5, target, new)))
            col[pl.ds(pl.multiple_of(i * 32, 32), 32), :] = new
            return carry

        lax.fori_loop(0, 8, step, None)
        stats.start(b, 0, col[...].T[:8])

    def settle(b):
        total = stats.total(b, 1)
        mine = hold[b, 0, stats.own(0)]
        t_lse = total[0:1] + jnp.log(total[1:2])
        s_lse = total[3:4] + jnp.log(total[4:5])
        row_kl = total[2:3] / total[1:2] - t_lse + s_lse
        row_nll = s_lse - total[5:6]
        masked = ex[0, 0:1, 0:1] + ex[1, 0:1, 0:1]
        weight = lossv[b, 1:2]
        lossv[b, 0:1] = weight * (row_kl + CE_WEIGHT * row_nll)
        scale = weight / masked
        a_s = (1.0 + CE_WEIGHT) * scale * jnp.exp(mine[3:4] - s_lse)
        a_t = scale * jnp.exp(mine[0:1] - t_lse)
        a_o = CE_WEIGHT * scale
        rows = jnp.concatenate([a_s, a_t, a_o, a_o, a_o, a_o, a_o, a_o], axis=0)
        coef[b] = jnp.concatenate([rows] * 16, axis=0).T

    for b in range(3):
        lossv[b, 1:2] = weights[:, b * 256 : b * 256 + 256]

    def student(b, carry):
        gather.whole(b)
        lhs = jnp.concatenate([ht[2 * b].reshape(3584, 128), ht[2 * b + 1].reshape(3584, 128)], axis=1)
        es[pl.ds(pl.multiple_of(b * 256, 256), 256), :] = lax.dot_general(
            lhs, sw[...], (((0,), (0,)), ((), ())), preferred_element_type=F32
        )
        pl.when(b >= 1)(lambda: stats.start(b - 1, 1, stats.total(b - 1, 0)))
        student_rows(b)
        pl.when(b == 2)(lambda: settle(0))
        return carry

    lax.fori_loop(0, 3, student, None)

    scatter = Scatter(place, pb, (rp, ra, rb, mid, rc, db), s_send, s_recv)

    def backward(b, carry):
        def grad_rows(i, carry):
            rows = pl.ds(pl.multiple_of(i * 32, 32), 32)
            full = pl.ds(pl.multiple_of(b * 256 + i * 32, 32), 32)
            a_s, a_t, a_o = (coef[b, rows, k : k + 1] for k in range(3))
            chosen = jnp.where(column == info[full, 0:1], a_o, 0.0)
            gb[rows, :] = (es[full, :] * a_s - et[full, :] * a_t - chosen).astype(BF16)
            return carry

        lax.fori_loop(0, 8, grad_rows, None)
        part = lax.dot_general(sw[...], gb[...], (((1,), (1,)), ((), ())), preferred_element_type=F32).astype(BF16)
        pb[b, 0] = part[:, :128].reshape(4, 4, 2, 112, 128)
        pb[b, 1] = part[:, 128:].reshape(4, 4, 2, 112, 128)
        scatter.start_pair(b)

        @pl.when(b == 0)
        def _():
            stats.start(2, 1, stats.total(2, 0))
            settle(1)

        @pl.when(b == 1)
        def _():
            scatter.lead_far(0)
            settle(2)

        @pl.when(b == 2)
        def _():
            scatter.lead_far(1)
            scatter.lead_near(0)

        return carry

    lax.fori_loop(0, 3, backward, None)
    part = lossv[0, 0:1] + lossv[1, 0:1] + lossv[2, 0:1]
    ex[2] = jnp.broadcast_to(jnp.sum(part, axis=1, keepdims=True), (8, 128))
    loss = send(ex.at[2], ex.at[3], ex_send.at[1], ex_recv.at[1], across)
    loss.start()
    scatter.lead_far(2)
    scatter.lead_near(1)
    scatter.second(0)
    scatter.lead_near(2)
    scatter.second(1)
    scatter.last(0)
    scatter.second(2)
    scatter.last(1)
    scatter.finish(0, out)
    scatter.last(2)
    scatter.finish(1, out)
    loss.wait()
    loss_out[...] = (ex[2] + ex[3]) / (ex[0] + ex[1])

    def tidy(b, carry):
        gather.drain(b)
        stats.drain(b)
        return carry

    lax.fori_loop(0, 3, tidy, None)
    for swap in swaps:
        swap.wait_send()
    scatter.finish(2, out)


def local(teacher_hidden, teacher_head, student_hidden, student_head, token_ids, response_mask):
    loss, grad = pl.pallas_call(
        kernel,
        out_shape=(jax.ShapeDtypeStruct((8, 128), F32), jax.ShapeDtypeStruct((56, 768), BF16)),
        in_specs=[ANY, ANY, VMEM, ANY, VMEM, VMEM],
        out_specs=(VMEM, VMEM),
        scratch_shapes=[
            pltpu.VMEM((768, 4096), BF16),
            pltpu.VMEM((4096, 1280), BF16),
            pltpu.VMEM((3584, 1280), BF16),
            pltpu.VMEM((6, 4, 4, 2, 112, 128), BF16),
            pltpu.VMEM((2, 3, 2, 64, 128), BF16),
            pltpu.VMEM((768, 1280), F32),
            pltpu.VMEM((768, 1280), F32),
            pltpu.VMEM((256, 1280), BF16),
            pltpu.VMEM((768, 128), F32),
            pltpu.VMEM((768, 128), F32),
            pltpu.VMEM((256, 128), F32),
            pltpu.VMEM((3, 256, 128), F32),
            pltpu.VMEM((3, 2, 8, 8, 256), F32),
            pltpu.VMEM((4, 8, 128), F32),
            pltpu.VMEM((3, 8, 256), F32),
            pltpu.VMEM((3, 2, 4, 4, 2, 112, 128), BF16),
            pltpu.VMEM((3, 4, 4, 2, 112, 128), BF16),
            pltpu.VMEM((3, 2, 4, 112, 128), BF16),
            pltpu.VMEM((3, 2, 4, 2, 112, 128), BF16),
            pltpu.VMEM((3, 4, 2, 112, 128), BF16),
            pltpu.VMEM((3, 7, 112, 128), BF16),
            pltpu.VMEM((3, 2, 112, 128), BF16),
            DMA((14,)),
            DMA((2, 3)),
            DMA((2,)),
            DMA((2,)),
            DMA((3, 11)),
            DMA((3, 11)),
            DMA((3, 5)),
            DMA((3, 5)),
            DMA((3, 2, 7)),
            DMA((3, 2, 7)),
            DMA((3, 13)),
            DMA((3, 13)),
        ],
        compiler_params=pltpu.CompilerParams(collective_id=0, has_side_effects=True, vmem_limit_bytes=LIMIT),
        name="distill",
    )(teacher_hidden, teacher_head, student_hidden.T, student_head, token_ids, response_mask)
    return loss[0, 0], grad.T


def solution(mesh):
    placed = (
        P("rows", None),
        P(None, "vocab"),
        P("rows", "vocab"),
        P(None, "vocab"),
        P("rows"),
        P("rows"),
    )
    return jax.shard_map(
        local, mesh=mesh, in_specs=placed, out_specs=(P(), P("rows", "vocab")), check_vma=False
    )
```

time: 889 us -> 84.8 us (0.10)
  blocking collectives: 418 us -> 0 us
  waiting for transfers between devices: 399 us -> 0 us
  Pallas kernels: 0 us -> 81.2 us
  matrix products: 43.6 us -> 0 us
  between operations: 16.6 us -> 0.64 us
    reduce_scatter x1 -> x0, waiting for transfers between devices: 300 us -> none  [local(): lax.psum_scatter(lax.dot_general(logit_grad, student_head, (((1,), (1,)),...]
    psum x2 -> x0, blocking collectives: 278 us -> none  [the longest x1 272 us: local(): lax.psum((jnp.sum(t_exp, axis=1), jnp.sum(t_exp * difference, axis=1), jn...]
    pmax x1 -> x0, blocking collectives: 140 us -> none  [local(): lax.pmax((jnp.max(teacher_logits, axis=1), jnp.max(student_logits, axis=1...]
    all_gather x1 -> x0, waiting for transfers between devices: 98.6 us -> none  [local(): whole_hidden = lax.all_gather(student_hidden, 'vocab', axis=1, tiled=True)]
    pallas_call x0 -> x1, Pallas kernels: none -> 81.2 us  [local(): pl.pallas_call(kernel, out_shape=(jax.ShapeDtypeStruct((8, 128), F32), ja...]
    dot_general x3 -> x0, matrix products: 43.6 us -> none  [the longest x1 15.4 us: local(): lax.dot_general(logit_grad, student_head, (((1,), (1,)), ((), ())), prefe...]
  transfers between devices with their start and end apart: 2 -> 0, of which waited for: 2 -> 0; matrix products, arithmetic and copies ran while one was open for 2% -> 0% of each run, Pallas kernels for 0% -> 0%
where the time goes in v2:
time: 84.8 us; the launch traced here: 84.6 us
  Pallas kernels  81.2 us (96%)
  local copies, waits for them, and re-layouts  2.72 us (3%)
    pallas_call x1, Pallas kernels, local(): pl.pallas_call(kernel, out_shape=(jax.ShapeDtypeStruct((8, 128), F32), ja...  81.2 us

profile of v2, /device:TPU:1, one launch (start us, length us, event | category | flops | bytes accessed | tf_op | source)
XLA Modules:
  0.0 84.6 jit_solution(11444151021122071086)
XLA Ops:
  0.6 81.2 %distill.1 = (f32[8,128]{1,0:T(8,128)}, bf16[56,768]{1,0:T(8,128)(2,1)}) custom-call(bf16[768,4096]{1,0:T(8,128)(2,1)} %th_hbm.1, bf16[4096,1280]{1,0:T(8,128)(2,1)} %tw_hbm.1, bf16[56,768]{1,0:T(8,128)(2,1)} %bitcast.3, bf16[3584,1280]{1,0:T(8,128)(2,1)} %sw_hbm.1, s32[768]{0:T(1024)} %tok.1, s32[768]{0:T(1024)} %mask.1), custom_call_target="tpu_custom_call" | custom-call | tf_op jit(solution)/shard_map/distill/pallas_call | solution.py:516
  81.9 1.2 %slice.3 = f32[1,1]{1,0:T(1,128)} slice(f32[8,128]{1,0:T(8,128)} %get-tuple-element.4), slice={[0:1], [0:1]} | slice | bytes 8 | tf_op jit(solution)/shard_map/slice | solution.py:560
  83.1 1.5 %copy.9 = bf16[768,56]{0,1:T(8,128)(2,1)} copy(bf16[768,56]{0,1:T(8,128)(2,1)} %bitcast.4) | data formatting | bytes 172032

commit v3 on v2

--- a/solution.py
+++ b/solution.py
@@ -8,6 +8,7 @@
 from jax.sharding import PartitionSpec as P
 
 CE_WEIGHT = 0.5
+STRIP = 64
 F32, BF16 = jnp.float32, jnp.bfloat16
 VMEM = pl.BlockSpec(memory_space=pltpu.VMEM)
 ANY = pl.BlockSpec(memory_space=pl.ANY)
@@ -80,26 +81,35 @@
         place = self.place
         f, g = place.own(core)
         w = functools.partial(piece, self.ht, (2 * b + core,), core)
-        if k < 7:
-            d, flip = SEVEN[k]
-            src, device = w(f, g, place.y), place.lead(core, d, flip)
-        else:
-            src, device = [
-                (w(ALL, g, ALL), place.other(core, 1)),
-                (w(ALL, g, ALL), place.other(core, 3)),
-                (w(ALL, (g + 3) % 4, 0), place.other(core, 1)),
-                (w(ALL, (g + 1) % 4, 1), place.other(core, 3)),
-            ][k - 7]
+        src, device = [
+            (w(f, g, place.y), place.at(flip_y=True)),
+            (w(f, g, ALL), place.lead(core, 1)),
+            (w(f, g, ALL), place.lead(core, 2)),
+            (w(f, g, ALL), place.lead(core, 3)),
+            (w(ALL, g, 0), place.other(core, 1)),
+            (w(ALL, g, 1), place.other(core, 3)),
+            (w(ALL, g, 1), place.other(core, 1)),
+            (w(ALL, g, 0), place.other(core, 3)),
+            (w(ALL, (g + 3) % 4, 0), place.other(core, 1)),
+            (w(ALL, (g + 1) % 4, 1), place.other(core, 3)),
+        ][k]
         return send(src, src, self.ss.at[b, k], self.rs.at[b, k], device)
 
     def landed(self, core, b, k):
         f, g = self.place.own(core)
         w = functools.partial(piece, self.ht, (2 * b + core,), core)
-        if k < 7:
-            d, flip = SEVEN[k]
-            slot = w((f + 4 - d) % 4, g, 1 - self.place.y if flip else self.place.y)
-        else:
-            slot = [w(ALL, (g + 3) % 4, ALL), w(ALL, (g + 1) % 4, ALL), w(ALL, (g + 2) % 4, 0), w(ALL, (g + 2) % 4, 1)][k - 7]
+        slot = [
+            w(f, g, 1 - self.place.y),
+            w((f + 3) % 4, g, ALL),
+            w((f + 2) % 4, g, ALL),
+            w((f + 1) % 4, g, ALL),
+            w(ALL, (g + 3) % 4, 0),
+            w(ALL, (g + 1) % 4, 1),
+            w(ALL, (g + 3) % 4, 1),
+            w(ALL, (g + 1) % 4, 0),
+            w(ALL, (g + 2) % 4, 0),
+            w(ALL, (g + 2) % 4, 1),
+        ][k]
         send(slot, slot, self.ss.at[b, k], self.rs.at[b, k], self.place.at(flip_c=True)).wait_recv()
 
     def relay(self, core, b, k):
@@ -115,36 +125,54 @@
         return send(slot, slot, self.relay_ss.at[b, k], self.relay_rs.at[b, k], self.place.at(flip_c=True))
 
     def first(self, b):
-        def step(core):
-            for k in range(7):
+        self.place.each_core(lambda core: self.copy(core, b, 0).start())
+
+    def line(self, b):
+        def step(core):
+            self.landed(core, b, 0)
+            for k in (1, 3, 2):
                 self.copy(core, b, k).start()
 
         self.place.each_core(step)
 
     def plane(self, b):
         def step(core):
-            for k in range(7):
+            for k in (1, 2, 3):
                 self.landed(core, b, k)
+            self.copy(core, b, 4).start()
+            self.copy(core, b, 5).start()
+            self.relay(core, b, 0).start()
+
+        self.place.each_core(step)
+
+    def plane_rest(self, b):
+        def step(core):
+            self.copy(core, b, 6).start()
             self.copy(core, b, 7).start()
-            self.copy(core, b, 8).start()
-            self.relay(core, b, 0).start()
 
         self.place.each_core(step)
 
     def onward(self, b):
         def step(core):
-            for k in (7, 8):
+            for k in (4, 5):
                 self.landed(core, b, k)
-                self.copy(core, b, k + 2).start()
-                self.relay(core, b, k - 6).start()
+                self.copy(core, b, k + 4).start()
+
+        self.place.each_core(step)
+
+    def rest(self, b):
+        def step(core):
+            for k in (6, 7):
+                self.landed(core, b, k)
+                self.relay(core, b, k - 5).start()
 
         self.place.each_core(step)
 
     def whole(self, b):
         def step(core):
-            for k in (9, 10):
+            for k in (8, 9):
                 self.landed(core, b, k)
-                self.relay(core, b, k - 6).start()
+                self.relay(core, b, k - 5).start()
             for k in range(5):
                 self.relay(1 - core, b, k).wait_recv()
 
@@ -152,7 +180,7 @@
 
     def drain(self, b):
         def step(core):
-            for k in range(11):
+            for k in range(10):
                 self.copy(core, b, k).wait_send()
             for k in range(5):
                 self.relay(core, b, k).wait_send()
@@ -226,24 +254,36 @@
             dst, device = self.rc.at[b, k - 5], place.other(core, d, flip)
         else:
             src, dst, device = {
-                0: lambda: (self.pb.at[b, 1 - core], self.rp.at[b], place.at(flip_c=True)),
+                0: lambda: (self.pb.at[b, 1 - core, 0:2], self.rp.at[b, 0:2], place.at(flip_c=True)),
+                13: lambda: (self.pb.at[b, 1 - core, 2:4], self.rp.at[b, 2:4], place.at(flip_c=True)),
                 1: lambda: (w((f + 2) % 4, ALL, 0), self.ra.at[b, 0], place.lead(core, 1)),
                 2: lambda: (w((f + 2) % 4, ALL, 1), self.ra.at[b, 1], place.lead(core, 3)),
-                3: lambda: (w((f + 1) % 4, ALL, ALL), self.rb.at[b, 0], place.lead(core, 1)),
-                4: lambda: (w((f + 3) % 4, ALL, ALL), self.rb.at[b, 1], place.lead(core, 3)),
+                3: lambda: (w((f + 1) % 4, ALL, 1), self.rb.at[b, 0, :, 1], place.lead(core, 1)),
+                4: lambda: (w((f + 3) % 4, ALL, 0), self.rb.at[b, 1, :, 0], place.lead(core, 3)),
+                14: lambda: (w((f + 1) % 4, ALL, 0), self.rb.at[b, 0, :, 0], place.lead(core, 1)),
+                15: lambda: (w((f + 3) % 4, ALL, 1), self.rb.at[b, 1, :, 1], place.lead(core, 3)),
                 12: lambda: (self.db.at[b, core], self.db.at[b, core], place.at(flip_c=True)),
             }[k]()
         return send(src, dst, self.ss.at[b, k], self.rs.at[b, k], device)
 
-    def start_pair(self, b):
-        self.place.each_core(lambda core: self.copy(core, b, 0).start())
+    def start_pair(self, b, half):
+        self.place.each_core(lambda core: self.copy(core, b, 13 * half).start())
+
+    def pair_sum(self, core, b, ahead):
+        f, g = self.place.own(core)
+        at = piece(self.pb, (b, core), core, (f + ahead) % 4, ALL, ALL)
+        theirs = piece(self.rp, (b,), core, (f + ahead) % 4, ALL, ALL)
+        return at, at[...].astype(F32) + theirs[...].astype(F32)
 
     def lead_far(self, b):
         def step(core):
             self.copy(core, b, 0).wait_recv()
-            self.pb[b, core] = (self.pb[b, core].astype(F32) + self.rp[b].astype(F32)).astype(BF16)
-            self.copy(core, b, 1).start()
-            self.copy(core, b, 2).start()
+            self.copy(core, b, 13).wait_recv()
+            for ahead in (2, 1, 3):
+                at, value = self.pair_sum(core, b, ahead)
+                at[...] = value.astype(BF16)
+                for k in {2: (1, 2), 1: (3,), 3: (4,)}[ahead]:
+                    self.copy(core, b, k).start()
 
         self.place.each_core(step)
 
@@ -254,17 +294,17 @@
                 self.copy(core, b, k).wait_recv()
                 at = piece(self.pb, (b, core), core, (f + ahead) % 4, ALL, y)
                 at[...] = (at[...].astype(F32) + self.ra[b, k - 1].astype(F32)).astype(BF16)
-                self.copy(core, b, k + 2).start()
+                self.copy(core, b, k + 13).start()
 
         self.place.each_core(step)
 
     def second(self, b):
         def step(core):
             f, g = self.place.own(core)
-            self.copy(core, b, 3).wait_recv()
-            self.copy(core, b, 4).wait_recv()
-            mine = piece(self.pb, (b, core), core, f, ALL, ALL)
-            self.mid[b] = (mine[...].astype(F32) + self.rb[b, 0].astype(F32) + self.rb[b, 1].astype(F32)).astype(BF16)
+            for k in (3, 4, 14, 15):
+                self.copy(core, b, k).wait_recv()
+            at, mine = self.pair_sum(core, b, 0)
+            self.mid[b] = (mine + self.rb[b, 0].astype(F32) + self.rb[b, 1].astype(F32)).astype(BF16)
             for k in range(5, 12):
                 self.copy(core, b, k).start()
 
@@ -287,7 +327,7 @@
         def step(core):
             slot = self.db.at[b, 1 - core]
             send(slot, slot, self.ss.at[b, 12], self.rs.at[b, 12], self.place.at(flip_c=True)).wait_recv()
-            for k in range(13):
+            for k in range(16):
                 self.copy(core, b, k).wait_send()
             for half in (0, 1):
                 mine = self.db[b, half].astype(F32)[core * 56 : core * 56 + 56]
@@ -340,7 +380,6 @@
     weights = mask[...].astype(F32).reshape(1, 768)
     ex[0] = jnp.broadcast_to(jnp.sum(weights, axis=1, keepdims=True), (8, 128))
     count = send(ex.at[0], ex.at[1], ex_send.at[0], ex_recv.at[0], across)
-    count.start()
     gather = Gather(place, ht, g_send, g_recv, r_send, r_recv)
 
     for b in range(3):
@@ -353,10 +392,13 @@
         ht[2 * b + place.c, place.x, place.z, place.y] = both.astype(BF16)
         gather.first(b)
 
+    count.start()
     first_col = lax.axis_index("vocab") * 1280
     local_tok = (tok[...] - first_col).astype(F32).reshape(1, 768)
     info[...] = jnp.broadcast_to(local_tok, (128, 768)).T
 
+    for b in range(3):
+        gather.line(b)
     for i in range(4):
         tw_load(i).wait()
 
@@ -364,55 +406,87 @@
         rows = pl.ds(pl.multiple_of(i * 128, 128), 128)
         th_load(i).wait()
         et[rows, :] = jnp.dot(th[rows, :], tw[...], preferred_element_type=F32)
-        pl.when(i == 2)(lambda: gather.plane(0))
-        pl.when(i == 3)(lambda: gather.plane(1))
-        pl.when(i == 4)(lambda: gather.plane(2))
-        pl.when(i == 5)(lambda: gather.onward(0))
+
+        @pl.when(i == 1)
+        def _():
+            gather.plane(0)
+            gather.plane_rest(0)
+
+        pl.when(i == 2)(lambda: gather.plane(1))
+
+        @pl.when(i == 3)
+        def _():
+            gather.onward(0)
+            gather.plane_rest(1)
+            gather.plane(2)
+
+        pl.when(i == 4)(lambda: gather.rest(0))
+
+        @pl.when(i == 5)
+        def _():
+            gather.onward(1)
+            gather.plane_rest(2)
+
         return carry
 
     lax.fori_loop(0, 6, teacher, None)
 
-    lane = lax.broadcasted_iota(jnp.int32, (32, 128), 1)
+    lane = lax.broadcasted_iota(jnp.int32, (STRIP, 128), 1)
+    strips = [slice(j * 128, j * 128 + 128) for j in range(10)]
+
+    def strip(i):
+        return pl.ds(pl.multiple_of(i * STRIP, STRIP), STRIP)
+
+    def row_max(ref, rows):
+        top = functools.reduce(jnp.maximum, [ref[rows, j] for j in strips])
+        return jnp.max(top, axis=1, keepdims=True)
+
+    def row_sum(value):
+        return jnp.sum(value, axis=1, keepdims=True)
 
     def teacher_rows(i, carry):
-        rows = pl.ds(pl.multiple_of(i * 32, 32), 32)
-        t = et[rows, :]
-        top = jnp.max(t, axis=1, keepdims=True)
-        e = jnp.exp(t - top)
-        et[rows, :] = e
-        total = jnp.sum(e, axis=1, keepdims=True)
-        mean = jnp.sum(e * t, axis=1, keepdims=True)
-        tcol[rows, :] = jnp.where(lane == 0, top, jnp.where(lane == 1, total, jnp.where(lane == 2, mean, 0.0)))
+        rows = strip(i)
+        top = row_max(et, rows)
+        total = mean = jnp.zeros((STRIP, 128), F32)
+        for j in strips:
+            t = et[rows, j]
+            e = jnp.exp(t - top)
+            et[rows, j] = e
+            total, mean = total + e, mean + e * t
+        tcol[rows, :] = jnp.where(
+            lane == 0, top, jnp.where(lane == 1, row_sum(total), jnp.where(lane == 2, row_sum(mean), 0.0))
+        )
         return carry
 
-    lax.fori_loop(0, 12, teacher_rows, None)
-    gather.onward(1)
-    lax.fori_loop(12, 24, teacher_rows, None)
-    gather.onward(2)
+    lax.fori_loop(0, 6, teacher_rows, None)
+    gather.rest(1)
+    lax.fori_loop(6, 12, teacher_rows, None)
     for i in range(4):
         sw_load(i).wait()
     count.wait()
 
     stats = Statistics(place, hold, st_send, st_recv)
-    column = lax.broadcasted_iota(jnp.int32, (32, 1280), 1).astype(F32)
+    column = lax.broadcasted_iota(jnp.int32, (STRIP, 128), 1).astype(F32)
 
     def student_rows(b):
         def step(i, carry):
-            rows = pl.ds(pl.multiple_of(b * 256 + i * 32, 32), 32)
-            s = es[rows, :]
-            top = jnp.max(s, axis=1, keepdims=True)
-            e = jnp.exp(s - top)
-            es[rows, :] = e
-            total = jnp.sum(e, axis=1, keepdims=True)
-            mean = jnp.sum(et[rows, :] * s, axis=1, keepdims=True)
-            target = jnp.sum(jnp.where(column == info[rows, 0:1], s, 0.0), axis=1, keepdims=True)
+            rows = strip(b * 4 + i)
+            top = row_max(es, rows)
+            token = info[rows, :]
+            total = mean = target = jnp.zeros((STRIP, 128), F32)
+            for j in strips:
+                s = es[rows, j]
+                e = jnp.exp(s - top)
+                es[rows, j] = e
+                total, mean = total + e, mean + et[rows, j] * s
+                target = target + jnp.where(column == token - j.start, s, 0.0)
             old = tcol[rows, :]
-            new = jnp.where(lane == 2, old - mean, old)
-            new = jnp.where(lane == 3, top, jnp.where(lane == 4, total, jnp.where(lane == 5, target, new)))
-            col[pl.ds(pl.multiple_of(i * 32, 32), 32), :] = new
+            new = jnp.where(lane == 2, old - row_sum(mean), old)
+            new = jnp.where(lane == 3, top, jnp.where(lane == 4, row_sum(total), jnp.where(lane == 5, row_sum(target), new)))
+            col[strip(i), :] = new
             return carry
 
-        lax.fori_loop(0, 8, step, None)
+        lax.fori_loop(0, 4, step, None)
         stats.start(b, 0, col[...].T[:8])
 
     def settle(b):
@@ -436,13 +510,15 @@
         lossv[b, 1:2] = weights[:, b * 256 : b * 256 + 256]
 
     def student(b, carry):
+        pl.when(b == 0)(lambda: gather.onward(2))
+        pl.when(b == 1)(lambda: gather.rest(2))
         gather.whole(b)
         lhs = jnp.concatenate([ht[2 * b].reshape(3584, 128), ht[2 * b + 1].reshape(3584, 128)], axis=1)
         es[pl.ds(pl.multiple_of(b * 256, 256), 256), :] = lax.dot_general(
             lhs, sw[...], (((0,), (0,)), ((), ())), preferred_element_type=F32
         )
+        student_rows(b)
         pl.when(b >= 1)(lambda: stats.start(b - 1, 1, stats.total(b - 1, 0)))
-        student_rows(b)
         pl.when(b == 2)(lambda: settle(0))
         return carry
 
@@ -450,39 +526,48 @@
 
     scatter = Scatter(place, pb, (rp, ra, rb, mid, rc, db), s_send, s_recv)
 
-    def backward(b, carry):
-        def grad_rows(i, carry):
-            rows = pl.ds(pl.multiple_of(i * 32, 32), 32)
-            full = pl.ds(pl.multiple_of(b * 256 + i * 32, 32), 32)
-            a_s, a_t, a_o = (coef[b, rows, k : k + 1] for k in range(3))
-            chosen = jnp.where(column == info[full, 0:1], a_o, 0.0)
-            gb[rows, :] = (es[full, :] * a_s - et[full, :] * a_t - chosen).astype(BF16)
+    def grad_rows(b):
+        def step(i, carry):
+            rows, full = strip(i), strip(b * 4 + i)
+            token = info[full, :]
+            a_s, a_t, a_o = (jnp.broadcast_to(coef[b, rows, k : k + 1], (STRIP, 128)) for k in range(3))
+            for j in strips:
+                chosen = jnp.where(column == token - j.start, a_o, 0.0)
+                gb[rows, j] = (es[full, j] * a_s - et[full, j] * a_t - chosen).astype(BF16)
             return carry
 
-        lax.fori_loop(0, 8, grad_rows, None)
-        part = lax.dot_general(sw[...], gb[...], (((1,), (1,)), ((), ())), preferred_element_type=F32).astype(BF16)
-        pb[b, 0] = part[:, :128].reshape(4, 4, 2, 112, 128)
-        pb[b, 1] = part[:, 128:].reshape(4, 4, 2, 112, 128)
-        scatter.start_pair(b)
-
-        @pl.when(b == 0)
+        lax.fori_loop(0, 4, step, None)
+
+    def backward(i, carry):
+        b, half = i // 2, i % 2
+        pl.when(half == 0)(lambda: grad_rows(b))
+        part = lax.dot_general(
+            sw[pl.ds(pl.multiple_of(half * 1792, 1792), 1792), :],
+            gb[...],
+            (((1,), (1,)), ((), ())),
+            preferred_element_type=F32,
+        ).astype(BF16)
+        pb[b, 0, pl.ds(half * 2, 2)] = part[:, :128].reshape(2, 4, 2, 112, 128)
+        pb[b, 1, pl.ds(half * 2, 2)] = part[:, 128:].reshape(2, 4, 2, 112, 128)
+        pl.when(half == 0)(lambda: scatter.start_pair(b, 0))
+        pl.when(half == 1)(lambda: scatter.start_pair(b, 1))
+
+        @pl.when(i == 1)
         def _():
             stats.start(2, 1, stats.total(2, 0))
             settle(1)
 
-        @pl.when(b == 1)
-        def _():
-            scatter.lead_far(0)
-            settle(2)
-
-        @pl.when(b == 2)
+        pl.when(i == 2)(lambda: scatter.lead_far(0))
+        pl.when(i == 3)(lambda: settle(2))
+
+        @pl.when(i == 4)
         def _():
             scatter.lead_far(1)
             scatter.lead_near(0)
 
         return carry
 
-    lax.fori_loop(0, 3, backward, None)
+    lax.fori_loop(0, 6, backward, None)
     part = lossv[0, 0:1] + lossv[1, 0:1] + lossv[2, 0:1]
     ex[2] = jnp.broadcast_to(jnp.sum(part, axis=1, keepdims=True), (8, 128))
     loss = send(ex.at[2], ex.at[3], ex_send.at[1], ex_recv.at[1], across)
@@ -510,6 +595,11 @@
     for swap in swaps:
         swap.wait_send()
     scatter.finish(2, out)
+
+
+def results_kernel(loss, grad, loss_out, grad_out):
+    loss_out[0, 0] = loss[0, 0]
+    grad_out[...] = grad[...]
 
 
 def local(teacher_hidden, teacher_head, student_hidden, student_head, token_ids, response_mask):
@@ -545,18 +635,25 @@
             DMA((2, 3)),
             DMA((2,)),
             DMA((2,)),
-            DMA((3, 11)),
-            DMA((3, 11)),
+            DMA((3, 10)),
+            DMA((3, 10)),
             DMA((3, 5)),
             DMA((3, 5)),
             DMA((3, 2, 7)),
             DMA((3, 2, 7)),
-            DMA((3, 13)),
-            DMA((3, 13)),
+            DMA((3, 16)),
+            DMA((3, 16)),
         ],
         compiler_params=pltpu.CompilerParams(collective_id=0, has_side_effects=True, vmem_limit_bytes=LIMIT),
         name="distill",
     )(teacher_hidden, teacher_head, student_hidden.T, student_head, token_ids, response_mask)
+    loss, grad = pl.pallas_call(
+        results_kernel,
+        out_shape=(jax.ShapeDtypeStruct((1, 1), F32), jax.ShapeDtypeStruct((56, 768), BF16)),
+        in_specs=[VMEM, VMEM],
+        out_specs=(pl.BlockSpec(memory_space=pltpu.SMEM), VMEM),
+        name="results",
+    )(loss, grad)
     return loss[0, 0], grad.T
 
 

time: 84.8 us -> 78.8 us (0.929)
  Pallas kernels: 81.2 us -> 78 us
  local copies, waits for them, and re-layouts: 2.72 us -> 0 us
    pallas_call x1, Pallas kernels: 81.2 us -> 76.4 us  [local(): pl.pallas_call(kernel, out_shape=(jax.ShapeDtypeStruct((8, 128), F32), ja...]
    pallas_call x0 -> x1, Pallas kernels: none -> 1.54 us  [local(): pl.pallas_call(results_kernel, out_shape=(jax.ShapeDtypeStruct((1, 1), F3...]
    unnamed x1 -> x0, local copies, waits for them, and re-layouts: 1.53 us -> none
    slice x1 -> x0, local copies, waits for them, and re-layouts: 1.19 us -> none  [local(): return (loss[0, 0], grad.T)]
where the time goes in v3:
time: 78.8 us; the launch traced here: 78.6 us
  Pallas kernels  78 us (99%)
    pallas_call x1, Pallas kernels, local(): pl.pallas_call(kernel, out_shape=(jax.ShapeDtypeStruct((8, 128), F32), ja...  76.4 us

profile of v3, /device:TPU:1, one launch (start us, length us, event | category | flops | bytes accessed | tf_op | source)
XLA Modules:
  0.0 78.6 jit_solution(6342132475230367660)
XLA Ops:
  0.6 76.4 %distill.1 = (f32[8,128]{1,0:T(8,128)}, bf16[56,768]{1,0:T(8,128)(2,1)}) custom-call(bf16[768,4096]{1,0:T(8,128)(2,1)} %th_hbm.1, bf16[4096,1280]{1,0:T(8,128)(2,1)} %tw_hbm.1, bf16[56,768]{1,0:T(8,128)(2,1)} %bitcast.3, bf16[3584,1280]{1,0:T(8,128)(2,1)} %sw_hbm.1, s32[768]{0:T(1024)} %tok.1, s32[768]{0:T(1024)} %mask.1), custom_call_target="tpu_custom_call" | custom-call | tf_op jit(solution)/shard_map/distill/pallas_call | solution.py:606
  77.0 1.5 %results.1 = (f32[1,1]{1,0:T(1,128)}, bf16[56,768]{1,0:T(8,128)(2,1)}) custom-call(f32[8,128]{1,0:T(8,128)} %get-tuple-element.6.loss, bf16[56,768]{1,0:T(8,128)(2,1)} %get-tuple-element.7.grad), custom_call_target="tpu_custom_call" | custom-call | tf_op jit(solution)/shard_map/results/pallas_call | solution.py:650

commit v4 on v3

--- a/solution.py
+++ b/solution.py
@@ -33,8 +33,11 @@
             [self.at(dx=d, flip_y=f) for d in (1, 2, 3) for f in (False, True)]
             + [self.at(dz=d, flip_y=f) for d in (1, 2, 3) for f in (False, True)]
             + [self.at(dx=d, flip_c=True) for d in (1, 2, 3)]
-            + [self.at(flip_y=True), self.at(flip_c=True)]
+            + self.square()
         )
+
+    def square(self):
+        return [self.at(flip_c=True), self.at(flip_y=True), self.at(flip_y=True, flip_c=True)]
 
     def each_core(self, step):
         for core in (0, 1):
@@ -82,7 +85,7 @@
         f, g = place.own(core)
         w = functools.partial(piece, self.ht, (2 * b + core,), core)
         src, device = [
-            (w(f, g, place.y), place.at(flip_y=True)),
+            None,
             (w(f, g, ALL), place.lead(core, 1)),
             (w(f, g, ALL), place.lead(core, 2)),
             (w(f, g, ALL), place.lead(core, 3)),
@@ -99,7 +102,7 @@
         f, g = self.place.own(core)
         w = functools.partial(piece, self.ht, (2 * b + core,), core)
         slot = [
-            w(f, g, 1 - self.place.y),
+            None,
             w((f + 3) % 4, g, ALL),
             w((f + 2) % 4, g, ALL),
             w((f + 1) % 4, g, ALL),
@@ -124,12 +127,8 @@
         ][k]
         return send(slot, slot, self.relay_ss.at[b, k], self.relay_rs.at[b, k], self.place.at(flip_c=True))
 
-    def first(self, b):
-        self.place.each_core(lambda core: self.copy(core, b, 0).start())
-
     def line(self, b):
         def step(core):
-            self.landed(core, b, 0)
             for k in (1, 3, 2):
                 self.copy(core, b, k).start()
 
@@ -180,7 +179,7 @@
 
     def drain(self, b):
         def step(core):
-            for k in range(10):
+            for k in range(1, 10):
                 self.copy(core, b, k).wait_send()
             for k in range(5):
                 self.relay(core, b, k).wait_send()
@@ -338,7 +337,7 @@
 
 def kernel(
     th_hbm, tw_hbm, hid, sw_hbm, tok, mask, loss_out, out,
-    th, tw, sw, ht, pair, et, es, gb, info, tcol, col, coef, hold, ex, lossv, pb, rp, ra, rb, mid, rc, db,
+    th, tw, sw, ht, pair, near, et, es, gb, info, tcol, col, coef, hold, ex, lossv, pb, rp, ra, rb, mid, rc, db,
     local_sem, pair_sems, ex_send, ex_recv, g_send, g_recv, r_send, r_recv, st_send, st_recv, s_send, s_recv,
 ):
     place = Place()
@@ -366,13 +365,13 @@
     mine = jnp.concatenate([hid[...].astype(F32), jnp.zeros((8, 768), F32)], axis=0).astype(BF16)
     for b in range(3):
         for half in (0, 1):
-            pair[0, b, half] = mine[:, b * 256 + half * 128 : b * 256 + half * 128 + 128]
+            pair[b, half] = mine[:, b * 256 + half * 128 : b * 256 + half * 128 + 128]
     pl.semaphore_wait(barrier, len(peers))
+    halves = [1 - place.c, place.c, 1 - place.c]
     swaps = [
-        send(
-            pair.at[0, b, 1 - place.c], pair.at[1, b, 1 - place.c], pair_sems.at[0, b], pair_sems.at[1, b], place.at(flip_c=True)
-        )
+        send(pair.at[b, halves[k]], near.at[k, b], pair_sems.at[0, k, b], pair_sems.at[1, k, b], device)
         for b in range(3)
+        for k, device in enumerate(place.square())
     ]
     for swap in swaps:
         swap.start()
@@ -382,23 +381,22 @@
     count = send(ex.at[0], ex.at[1], ex_send.at[0], ex_recv.at[0], across)
     gather = Gather(place, ht, g_send, g_recv, r_send, r_recv)
 
+    def joined(mine, theirs):
+        mine, theirs = mine.astype(F32)[:56], theirs.astype(F32)[:56]
+        first = place.c == 0
+        return jnp.concatenate([jnp.where(first, mine, theirs), jnp.where(first, theirs, mine)], axis=0).astype(BF16)
+
     for b in range(3):
-        slot = pair.at[1, b, place.c]
-        send(slot, slot, pair_sems.at[0, b], pair_sems.at[1, b], place.at(flip_c=True)).wait_recv()
-        own = pair[0, b, place.c].astype(F32)[:56]
-        theirs = pair[1, b, place.c].astype(F32)[:56]
-        first = place.c == 0
-        both = jnp.concatenate([jnp.where(first, own, theirs), jnp.where(first, theirs, own)], axis=0)
-        ht[2 * b + place.c, place.x, place.z, place.y] = both.astype(BF16)
-        gather.first(b)
-
+        for k in range(3):
+            swaps[3 * b + k].wait_recv()
+        ht[2 * b + place.c, place.x, place.z, place.y] = joined(pair[b, place.c], near[0, b])
+        ht[2 * b + place.c, place.x, place.z, 1 - place.y] = joined(near[1, b], near[2, b])
+        gather.line(b)
     count.start()
     first_col = lax.axis_index("vocab") * 1280
     local_tok = (tok[...] - first_col).astype(F32).reshape(1, 768)
     info[...] = jnp.broadcast_to(local_tok, (128, 768)).T
 
-    for b in range(3):
-        gather.line(b)
     for i in range(4):
         tw_load(i).wait()
 
@@ -458,9 +456,9 @@
         )
         return carry
 
-    lax.fori_loop(0, 6, teacher_rows, None)
+    lax.fori_loop(0, 6, teacher_rows, None, unroll=2)
     gather.rest(1)
-    lax.fori_loop(6, 12, teacher_rows, None)
+    lax.fori_loop(6, 12, teacher_rows, None, unroll=2)
     for i in range(4):
         sw_load(i).wait()
     count.wait()
@@ -486,7 +484,7 @@
             col[strip(i), :] = new
             return carry
 
-        lax.fori_loop(0, 4, step, None)
+        lax.fori_loop(0, 4, step, None, unroll=True)
         stats.start(b, 0, col[...].T[:8])
 
     def settle(b):
@@ -536,7 +534,7 @@
                 gb[rows, j] = (es[full, j] * a_s - et[full, j] * a_t - chosen).astype(BF16)
             return carry
 
-        lax.fori_loop(0, 4, step, None)
+        lax.fori_loop(0, 4, step, None, unroll=True)
 
     def backward(i, carry):
         b, half = i // 2, i % 2
@@ -613,7 +611,8 @@
             pltpu.VMEM((4096, 1280), BF16),
             pltpu.VMEM((3584, 1280), BF16),
             pltpu.VMEM((6, 4, 4, 2, 112, 128), BF16),
-            pltpu.VMEM((2, 3, 2, 64, 128), BF16),
+            pltpu.VMEM((3, 2, 64, 128), BF16),
+            pltpu.VMEM((3, 3, 64, 128), BF16),
             pltpu.VMEM((768, 1280), F32),
             pltpu.VMEM((768, 1280), F32),
             pltpu.VMEM((256, 1280), BF16),
@@ -632,7 +631,7 @@
             pltpu.VMEM((3, 7, 112, 128), BF16),
             pltpu.VMEM((3, 2, 112, 128), BF16),
             DMA((14,)),
-            DMA((2, 3)),
+            DMA((2, 3, 3)),
             DMA((2,)),
             DMA((2,)),
             DMA((3, 10)),

time: 78.8 us -> 76.7 us (0.973)
  Pallas kernels: 78 us -> 75.9 us
    pallas_call x1, Pallas kernels: 76.4 us -> 74.4 us  [local(): pl.pallas_call(kernel, out_shape=(jax.ShapeDtypeStruct((8, 128), F32), ja...]
where the time goes in v4:
time: 76.7 us; the launch traced here: 76.6 us
  Pallas kernels  75.9 us (99%)
    pallas_call x1, Pallas kernels, local(): pl.pallas_call(kernel, out_shape=(jax.ShapeDtypeStruct((8, 128), F32), ja...  74.4 us
    pallas_call x1, Pallas kernels, local(): pl.pallas_call(results_kernel, out_shape=(jax.ShapeDtypeStruct((1, 1), F3...  1.54 us

profile of v4, /device:TPU:1, one launch (start us, length us, event | category | flops | bytes accessed | tf_op | source)
XLA Modules:
  0.0 76.6 jit_solution(3390322209056512584)
XLA Ops:
  0.6 74.4 %distill.1 = (f32[8,128]{1,0:T(8,128)}, bf16[56,768]{1,0:T(8,128)(2,1)}) custom-call(bf16[768,4096]{1,0:T(8,128)(2,1)} %th_hbm.1, bf16[4096,1280]{1,0:T(8,128)(2,1)} %tw_hbm.1, bf16[56,768]{1,0:T(8,128)(2,1)} %bitcast.3, bf16[3584,1280]{1,0:T(8,128)(2,1)} %sw_hbm.1, s32[768]{0:T(1024)} %tok.1, s32[768]{0:T(1024)} %mask.1), custom_call_target="tpu_custom_call" | custom-call | tf_op jit(solution)/shard_map/distill/pallas_call | solution.py:604
  75.0 1.5 %results.1 = (f32[1,1]{1,0:T(1,128)}, bf16[56,768]{1,0:T(8,128)(2,1)}) custom-call(f32[8,128]{1,0:T(8,128)} %get-tuple-element.6.loss, bf16[56,768]{1,0:T(8,128)(2,1)} %get-tuple-element.7.grad), custom_call_target="tpu_custom_call" | custom-call | tf_op jit(solution)/shard_map/results/pallas_call | solution.py:649

commit v5 on v4

--- a/solution.py
+++ b/solution.py
@@ -8,7 +8,7 @@
 from jax.sharding import PartitionSpec as P
 
 CE_WEIGHT = 0.5
-STRIP = 64
+STRIP = 128
 F32, BF16 = jnp.float32, jnp.bfloat16
 VMEM = pl.BlockSpec(memory_space=pltpu.VMEM)
 ANY = pl.BlockSpec(memory_space=pl.ANY)
@@ -302,10 +302,14 @@
             f, g = self.place.own(core)
             for k in (3, 4, 14, 15):
                 self.copy(core, b, k).wait_recv()
-            at, mine = self.pair_sum(core, b, 0)
-            self.mid[b] = (mine + self.rb[b, 0].astype(F32) + self.rb[b, 1].astype(F32)).astype(BF16)
-            for k in range(5, 12):
-                self.copy(core, b, k).start()
+            mine = piece(self.pb, (b, core), core, f, ALL, ALL)
+            theirs = piece(self.rp, (b,), core, f, ALL, ALL)
+            for d, ks in ((2, (10, 11)), (1, (5, 8)), (3, (6, 9)), (0, (7,))):
+                to = (g + d) % 4
+                parts = (mine[to], theirs[to], self.rb[b, 0, to], self.rb[b, 1, to])
+                self.mid[b, to] = sum(part.astype(F32) for part in parts).astype(BF16)
+                for k in ks:
+                    self.copy(core, b, k).start()
 
         self.place.each_core(step)
 
@@ -456,9 +460,9 @@
         )
         return carry
 
-    lax.fori_loop(0, 6, teacher_rows, None, unroll=2)
+    lax.fori_loop(0, 3, teacher_rows, None)
     gather.rest(1)
-    lax.fori_loop(6, 12, teacher_rows, None, unroll=2)
+    lax.fori_loop(3, 6, teacher_rows, None)
     for i in range(4):
         sw_load(i).wait()
     count.wait()
@@ -468,7 +472,7 @@
 
     def student_rows(b):
         def step(i, carry):
-            rows = strip(b * 4 + i)
+            rows = strip(b * 2 + i)
             top = row_max(es, rows)
             token = info[rows, :]
             total = mean = target = jnp.zeros((STRIP, 128), F32)
@@ -484,7 +488,7 @@
             col[strip(i), :] = new
             return carry
 
-        lax.fori_loop(0, 4, step, None, unroll=True)
+        lax.fori_loop(0, 2, step, None, unroll=True)
         stats.start(b, 0, col[...].T[:8])
 
     def settle(b):
@@ -508,14 +512,14 @@
         lossv[b, 1:2] = weights[:, b * 256 : b * 256 + 256]
 
     def student(b, carry):
-        pl.when(b == 0)(lambda: gather.onward(2))
-        pl.when(b == 1)(lambda: gather.rest(2))
         gather.whole(b)
         lhs = jnp.concatenate([ht[2 * b].reshape(3584, 128), ht[2 * b + 1].reshape(3584, 128)], axis=1)
         es[pl.ds(pl.multiple_of(b * 256, 256), 256), :] = lax.dot_general(
             lhs, sw[...], (((0,), (0,)), ((), ())), preferred_element_type=F32
         )
+        pl.when(b == 0)(lambda: gather.onward(2))
         student_rows(b)
+        pl.when(b == 0)(lambda: gather.rest(2))
         pl.when(b >= 1)(lambda: stats.start(b - 1, 1, stats.total(b - 1, 0)))
         pl.when(b == 2)(lambda: settle(0))
         return carry
@@ -526,7 +530,7 @@
 
     def grad_rows(b):
         def step(i, carry):
-            rows, full = strip(i), strip(b * 4 + i)
+            rows, full = strip(i), strip(b * 2 + i)
             token = info[full, :]
             a_s, a_t, a_o = (jnp.broadcast_to(coef[b, rows, k : k + 1], (STRIP, 128)) for k in range(3))
             for j in strips:
@@ -534,7 +538,7 @@
                 gb[rows, j] = (es[full, j] * a_s - et[full, j] * a_t - chosen).astype(BF16)
             return carry
 
-        lax.fori_loop(0, 4, step, None, unroll=True)
+        lax.fori_loop(0, 2, step, None, unroll=True)
 
     def backward(i, carry):
         b, half = i // 2, i % 2

time: 76.7 us -> 76 us (level)
  Pallas kernels: 75.9 us -> 75.1 us
    pallas_call x1, Pallas kernels: 74.4 us -> 73.6 us  [local(): pl.pallas_call(kernel, out_shape=(jax.ShapeDtypeStruct((8, 128), F32), ja...]
where the time goes in v5:
time: 76 us; the launch traced here: 75.8 us
  Pallas kernels  75.1 us (99%)
    pallas_call x1, Pallas kernels, local(): pl.pallas_call(kernel, out_shape=(jax.ShapeDtypeStruct((8, 128), F32), ja...  73.6 us
    pallas_call x1, Pallas kernels, local(): pl.pallas_call(results_kernel, out_shape=(jax.ShapeDtypeStruct((1, 1), F3...  1.54 us

profile of v5, /device:TPU:1, one launch (start us, length us, event | category | flops | bytes accessed | tf_op | source)
XLA Modules:
  0.0 75.8 jit_solution(5313292371630607801)
XLA Ops:
  0.6 73.6 %distill.1 = (f32[8,128]{1,0:T(8,128)}, bf16[56,768]{1,0:T(8,128)(2,1)}) custom-call(bf16[768,4096]{1,0:T(8,128)(2,1)} %th_hbm.1, bf16[4096,1280]{1,0:T(8,128)(2,1)} %tw_hbm.1, bf16[56,768]{1,0:T(8,128)(2,1)} %bitcast.3, bf16[3584,1280]{1,0:T(8,128)(2,1)} %sw_hbm.1, s32[768]{0:T(1024)} %tok.1, s32[768]{0:T(1024)} %mask.1), custom_call_target="tpu_custom_call" | custom-call | tf_op jit(solution)/shard_map/distill/pallas_call | solution.py:608
  74.2 1.5 %results.1 = (f32[1,1]{1,0:T(1,128)}, bf16[56,768]{1,0:T(8,128)(2,1)}) custom-call(f32[8,128]{1,0:T(8,128)} %get-tuple-element.6.loss, bf16[56,768]{1,0:T(8,128)(2,1)} %get-tuple-element.7.grad), custom_call_target="tpu_custom_call" | custom-call | tf_op jit(solution)/shard_map/results/pallas_call | solution.py:653
